TPU v7x, 32 devices: a whole 2x2x4 slice. The times are simulated.
32 devices in a mesh: rep: 2 (over y), exp: 16 (over z, x, core).
Axes of the slice: x: 2, y: 2, z: 4, core: 2. Of those that a mesh axis runs over, the one named last changes fastest.
Arguments:
- tokens: bfloat16 [4096, 3584], P(('rep', 'exp')), may hold values from -6 to 6
- cotangent: bfloat16 [4096, 3584], P(('rep', 'exp')), may hold values from -0.29882812 to 0.29882812
- gates: float32 [4096, 1], P(('rep', 'exp')), may hold values from 0.2 to 1.5
- routes: int32 [4096, 1], P(('rep', 'exp')), may hold values from 0 to 3; in each aligned block of 128 rows (0 to 127, 128 to 255, ...) at most 36 rows name the same one
- w_up: bfloat16 [14336, 1024], P(('exp', 'rep')), may hold values from -0.09375 to 0.09375
- w_down_t: bfloat16 [14336, 1024], P(('exp', 'rep')), may hold values from -0.1875 to 0.1875
Outputs:
- grad_tokens: bfloat16 [4096, 3584], P(('rep', 'exp'))
- grad_gates: float32 [4096, 1], P(('rep', 'exp'))
- grad_up: float32 [14336, 1024], P(('exp', 'rep'))
- grad_down_t: float32 [14336, 1024], P(('exp', 'rep'))
Inputs may be any that keep to these rules, and one draw needn't show every extreme that they name: `routes`: each row names one expert (1 = 1). Among the rows of one device no expert is named more than 36 times, and in every draw some expert is named exactly 36 times by the rows of some device.
All inputs are finite; a program needn't handle non-finite values.
Results may differ from a plain program's by a relative error of at most 0.012.
Values may be sent and summed in bfloat16 or wider, within the bound.
A program may use at most 64 MiB of HBM per device.

v0:
```python
import jax
import jax.numpy as jnp
from jax import lax
from jax.sharding import PartitionSpec as P

SLICES = 4


def swapped(x, axis, distance):
    return lax.ppermute(x, axis, [(i, i ^ 1 << distance) for i in range(lax.axis_size(axis))])


def contract_last(left_side, right_side):
    return lax.dot_general(
        left_side, right_side, (((1,), (1,)), ((), ())), preferred_element_type=jnp.float32
    )


def contract_first(left_side, right_side):
    return lax.dot_general(
        left_side, right_side, (((0,), (0,)), ((), ())), preferred_element_type=jnp.float32
    )


def shards(tokens, cotangent, gates, routes, w_up, w_down_t):
    tok_dev, top_count = routes.shape
    model_width = tokens.shape[1]
    piece_width = model_width // SLICES
    slice_bits = SLICES.bit_length() - 1
    n_devices = lax.axis_size("exp")
    experts = n_devices // SLICES
    capacity = min(tok_dev, max(2, 9 * tok_dev * top_count // (8 * experts)))
    slot_rows = capacity * n_devices
    exp_index = lax.axis_index("exp")
    up_rows, down_rows = (
        lax.all_gather(w_up, "rep", axis=0, tiled=True),
        lax.all_gather(w_down_t, "rep", axis=0, tiled=True),
    )
    flat_route = routes.reshape(-1)
    choice_count = flat_route.shape[0]
    onehot = (flat_route[:, None] == jnp.arange(experts, dtype=jnp.int32)[None, :]).astype(
        jnp.int32
    )
    earlier = jnp.cumsum(onehot, axis=0) - onehot
    slot_index = jnp.sum(earlier * onehot, axis=1)
    position = slot_index * experts + flat_route
    matches = position[None, :] == jnp.arange(capacity * experts, dtype=jnp.int32)[:, None]
    filled = jnp.any(matches, axis=1)
    chosen = jnp.sum(
        jnp.where(matches, jnp.arange(choice_count, dtype=jnp.int32)[None, :], 0), axis=1
    )
    source_row = chosen // top_count
    weight = gates.reshape(-1)[chosen]
    inputs_buf = jnp.where(filled[:, None], tokens[source_row], jnp.zeros((), tokens.dtype))
    inputs_buf = inputs_buf.reshape(capacity, n_devices, piece_width)
    grads_buf = jnp.where(
        filled[:, None], weight[:, None] * cotangent[source_row].astype(jnp.float32), 0.0
    )
    grads_buf = grads_buf.astype(jnp.bfloat16).reshape(capacity, n_devices, piece_width)
    inputs_in = lax.all_to_all(inputs_buf, "exp", split_axis=1, concat_axis=1, tiled=True)
    x_rows = inputs_in.reshape(slot_rows, piece_width)
    partial_value = jnp.dot(x_rows, up_rows, preferred_element_type=jnp.float32).astype(
        jnp.bfloat16
    )
    stacked = partial_value[None]
    for bit_number in range(slice_bits):
        upper_side = exp_index >> bit_number & 1 == 1
        half_width = stacked.shape[2] // 2
        lower_half = stacked[:, :, :half_width]
        upper_half = stacked[:, :, half_width:]
        kept_half = jnp.where(upper_side, upper_half, lower_half)
        given_half = jnp.where(upper_side, lower_half, upper_half)
        stacked = jnp.concatenate([kept_half, swapped(given_half, "exp", bit_number)], axis=0)
    activation = jnp.sum(stacked.astype(jnp.float32), axis=0)
    gating = jax.nn.sigmoid(activation)
    hidden_act = (activation * gating).astype(jnp.bfloat16)
    for bit_number in reversed(range(slice_bits)):
        upper_side = exp_index >> bit_number & 1 == 1
        partner_cols = swapped(hidden_act, "exp", bit_number)
        hidden_act = jnp.where(
            upper_side,
            jnp.concatenate([partner_cols, hidden_act], axis=1),
            jnp.concatenate([hidden_act, partner_cols], axis=1),
        )
    out_rows = contract_last(hidden_act, down_rows).astype(jnp.bfloat16)
    out_buf = out_rows.reshape(capacity, n_devices, piece_width)
    out_back = lax.all_to_all(out_buf, "exp", split_axis=1, concat_axis=1, tiled=True)
    grads_in = lax.all_to_all(grads_buf, "exp", split_axis=1, concat_axis=1, tiled=True)
    d_rows = grads_in.reshape(slot_rows, piece_width)
    grad_partial = jnp.dot(d_rows, down_rows, preferred_element_type=jnp.float32).astype(
        jnp.bfloat16
    )
    grad_stack = grad_partial[None]
    for bit_number in range(slice_bits):
        upper_side = exp_index >> bit_number & 1 == 1
        half_width = grad_stack.shape[2] // 2
        lower_half = grad_stack[:, :, :half_width]
        upper_half = grad_stack[:, :, half_width:]
        kept_half = jnp.where(upper_side, upper_half, lower_half)
        given_half = jnp.where(upper_side, lower_half, upper_half)
        grad_stack = jnp.concatenate([kept_half, swapped(given_half, "exp", bit_number)], axis=0)
    grad_cols = jnp.sum(grad_stack.astype(jnp.float32), axis=0)
    act_grad = (grad_cols * gating * (1.0 + activation * (1.0 - gating))).astype(jnp.bfloat16)
    for bit_number in reversed(range(slice_bits)):
        upper_side = exp_index >> bit_number & 1 == 1
        partner_cols = swapped(act_grad, "exp", bit_number)
        act_grad = jnp.where(
            upper_side,
            jnp.concatenate([partner_cols, act_grad], axis=1),
            jnp.concatenate([act_grad, partner_cols], axis=1),
        )
    dx_rows = contract_last(act_grad, up_rows).astype(jnp.bfloat16)
    dx_buf = dx_rows.reshape(capacity, n_devices, piece_width)
    up_term = contract_first(x_rows, act_grad)
    down_term = contract_first(d_rows, hidden_act)
    weight_sums = lax.psum_scatter(
        jnp.concatenate([up_term, down_term], axis=1).astype(jnp.bfloat16),
        "rep",
        scatter_dimension=0,
        tiled=True,
    ).astype(jnp.float32)
    hidden = up_rows.shape[1]
    grad_up = weight_sums[:, :hidden]
    grad_down_t = weight_sums[:, hidden:]
    dx_back = lax.all_to_all(dx_buf, "exp", split_axis=1, concat_axis=1, tiled=True)
    out_table = out_back.reshape(capacity * experts, model_width)
    dx_table = dx_back.reshape(capacity * experts, model_width)
    picked = out_table[position].astype(jnp.float32)
    repeated = jnp.repeat(cotangent, top_count, axis=0).astype(jnp.float32)
    grad_gates = jnp.sum(repeated * picked, axis=1).reshape(tok_dev, top_count)
    grad_tokens = jnp.sum(
        dx_table[position].astype(jnp.float32).reshape(tok_dev, top_count, model_width), axis=1
    )
    return (grad_tokens.astype(jnp.bfloat16), grad_gates, grad_up, grad_down_t)


def solution(mesh):
    placed = (
        P(("rep", "exp"), None),
        P(("rep", "exp"), None),
        P(("rep", "exp"), None),
        P(("rep", "exp"), None),
        P(("exp", "rep"), None),
        P(("exp", "rep"), None),
    )
    return jax.shard_map(
        shards,
        mesh=mesh,
        in_specs=placed,
        out_specs=(
            P(("rep", "exp"), None),
            P(("rep", "exp"), None),
            P(("exp", "rep"), None),
            P(("exp", "rep"), None),
        ),
        check_vma=False,
    )
```

profile of v0, /device:TPU:0, one launch (start us, length us, event | category | flops | bytes accessed | tf_op | source)
XLA Modules:
  0.0 233.4 jit_solution(2023622750038632332)
XLA Ops:
  7.2 0.8 fusion.7
  8.0 0.2 reduce_window_sum.11
  8.2 0.8 select_reduce_fusion.1
  9.0 0.7 multiply_add_fusion
  9.8 0.1 fusion.6
  9.9 2.2 gather_fusion.2
  12.1 1.7 gather.20
  14.1 1.3 copy_select_fusion
  15.4 7.5 %all-to-all-start.1 = ((bf16[36,16,896]{2,0,1:T(8,128)(2,1)}), bf16[36,16,896]{2,0,1:T(8,128)(2,1)S(1)}, u32[]{:S(2)}, u32[]{:S(2)}) async-start(bf16[36,16,896]{2,0,1:T(8,128)(2,1)} %copy_select_fusion), calls=%async_computation.1 | async-start | bytes 2293760 | tf_op jit(solution)/shard_map/all_to_all | solution.py:60
  22.9 0.7 all-gather.5.cloned.1.call-update
  23.6 2.2 gather_fusion.1
  25.8 2.7 %reshape.95 = f32[36,16,896]{2,1,0:T(8,128)} reshape(bf16[144,3584]{1,0:T(8,128)(2,1)} %gather_fusion.1) | data formatting | bytes 3096576 | tf_op jit(solution)/shard_map/convert_element_type | solution.py:57
  28.5 1.5 gather_fusion
  30.3 3.3 %fusion.1 = bf16[36,16,896]{2,0,1:T(8,128)(2,1)} fusion(f32[36,16,896]{2,1,0:T(8,128)} %reshape.95, f32[36,16]{0,1:T(8,128)S(1)} %bitcast.37, pred[36,16]{0,1:T(8,128)(4,1)S(1)} %bitcast.39), kind=kLoop, calls=%fused_computation.10 | loop fusion | flops 1548288 | bytes 3099456 | tf_op jit(solution)/shard_map/convert_element_type | solution.py:59
  33.6 13.9 %all-to-all-done.1 = bf16[36,16,896]{2,0,1:T(8,128)(2,1)S(1)} async-done(((bf16[36,16,896]{2,0,1:T(8,128)(2,1)}), bf16[36,16,896]{2,0,1:T(8,128)(2,1)S(1)}, u32[]{:S(2)}, u32[]{:S(2)}) %all-to-all-start.1) | async-done | bytes 1032224 | tf_op jit(solution)/shard_map/all_to_all | solution.py:60
  47.4 7.4 %all-to-all-start = ((bf16[36,16,896]{2,0,1:T(8,128)(2,1)}), bf16[36,16,896]{2,0,1:T(8,128)(2,1)}, u32[]{:S(2)}, u32[]{:S(2)}) async-start(bf16[36,16,896]{2,0,1:T(8,128)(2,1)} %fusion.1), calls=%async_computation | async-start | bytes 2293760 | tf_op jit(solution)/shard_map/all_to_all | solution.py:88
  54.9 0.7 all-gather.3.cloned.1.call-update
  55.6 0.2 reduce-scatter.2.cloned.1.call-start
  55.8 1.1 copy.37
  56.9 3.2 %fusion.3 = bf16[1,576,1024]{2,1,0:T(8,128)(2,1)S(1)} fusion(bf16[576,896]{1,0:T(8,128)(2,1)} %bitcast.31, bf16[896,1024]{1,0:T(8,128)(2,1)} %all-gather.5.cloned.1.call-done), kind=kOutput, calls=%fused_computation.19 | convolution fusion | flops 1057554432 | bytes 4046848 | tf_op jit(solution)/shard_map/dot_general | solution.py:62
  60.1 0.9 broadcast_select_fusion.1
  61.0 0.4 collective-permute-start.2
  61.4 18.1 %all-to-all-done = bf16[36,16,896]{2,0,1:T(8,128)(2,1)} async-done(((bf16[36,16,896]{2,0,1:T(8,128)(2,1)}), bf16[36,16,896]{2,0,1:T(8,128)(2,1)}, u32[]{:S(2)}, u32[]{:S(2)}) %all-to-all-start) | async-done | bytes 1032224 | tf_op jit(solution)/shard_map/all_to_all | solution.py:88
  79.5 1.4 copy.35
  80.9 7.9 %all-gather.3.cloned.1.call-done = bf16[896,1024]{1,0:T(8,128)(2,1)} async-done(((bf16[448,1024]{1,0:T(8,128)(2,1)}), bf16[896,1024]{1,0:T(8,128)(2,1)}) %all-gather.3.cloned.1.call-update) | async-done | bytes 1835024 | tf_op jit(solution)/shard_map/all_gather | solution.py:37
  88.7 2.9 %fusion.2 = bf16[1,576,1024]{2,1,0:T(8,128)(2,1)S(1)} fusion(bf16[576,896]{1,0:T(8,128)(2,1)S(1)} %bitcast.33, bf16[896,1024]{1,0:T(8,128)(2,1)} %all-gather.3.cloned.1.call-done), kind=kOutput, calls=%fused_computation.18 | convolution fusion | flops 1057554432 | bytes 4046848 | tf_op jit(solution)/shard_map/dot_general | solution.py:90
  91.6 0.9 broadcast_select_fusion.3
  92.5 1.4 broadcast_select_fusion.5
  93.9 1.5 collective-permute-start.3
  95.5 1.4 broadcast_select_fusion.7
  96.8 0.9 collective-permute-start.1
  97.8 12.3 %collective-permute-done.3 = bf16[2,576,256]{2,1,0:T(8,128)(2,1)S(1)} collective-permute-done((bf16[2,576,256]{2,1,0:T(8,128)(2,1)S(1)}, bf16[2,576,256]{2,1,0:T(8,128)(2,1)S(1)}, u32[]{:S(2)}, u32[]{:S(2)}) %collective-permute-start.3) | collective-permute-done | bytes 589856 | tf_op jit(solution)/shard_map/ppermute | solution.py:10
  110.1 0.2 convert_reduce_fusion
  110.3 12.1 %collective-permute-done.1 = bf16[2,576,256]{2,1,0:T(8,128)(2,1)S(1)} collective-permute-done((bf16[2,576,256]{2,1,0:T(8,128)(2,1)S(1)}, bf16[2,576,256]{2,1,0:T(8,128)(2,1)S(1)}, u32[]{:S(2)}, u32[]{:S(2)}) %collective-permute-start.1) | collective-permute-done | bytes 589856 | tf_op jit(solution)/shard_map/ppermute | solution.py:10
  122.4 0.2 convert_reduce_fusion.1
  122.6 0.3 multiply_convert_fusion
  122.8 1.5 collective-permute-start.6
  124.4 0.6 collective-permute-start.4
  124.9 7.9 %collective-permute-done.6 = bf16[576,256]{1,0:T(8,128)(2,1)S(1)} collective-permute-done((bf16[576,256]{1,0:T(8,128)(2,1)S(1)}, bf16[576,256]{1,0:T(8,128)(2,1)S(1)}, u32[]{:S(2)}, u32[]{:S(2)}) %collective-permute-start.6) | collective-permute-done | bytes 294944 | tf_op jit(solution)/shard_map/ppermute | solution.py:10
  132.8 0.2 maximum_select_fusion.3
  133.1 4.8 %collective-permute-done.4 = bf16[576,256]{1,0:T(8,128)(2,1)S(1)} collective-permute-done((bf16[576,256]{1,0:T(8,128)(2,1)S(1)}, bf16[576,256]{1,0:T(8,128)(2,1)S(1)}, u32[]{:S(2)}, u32[]{:S(2)}) %collective-permute-start.4) | collective-permute-done | bytes 294944 | tf_op jit(solution)/shard_map/ppermute | solution.py:10
  137.9 0.2 maximum_select_fusion.2
  138.2 1.7 convolution_convert_fusion
  139.8 0.3 collective-permute-done.5
  140.1 0.8 copy-done.9
  140.9 1.7 convolution_convert_fusion.1
  142.6 2.1 pad_maximum_fusion
  144.7 1.0 copy-done.10
  145.8 2.9 %convolution_convert_fusion.5 = bf16[576,896]{1,0:T(8,128)(2,1)S(1)} fusion(bf16[896,1024]{1,0:T(8,128)(2,1)} %all-gather.5.cloned.1.call-done, bf16[576,512]{1,0:T(8,128)(2,1)S(1)} %maximum_select_fusion.2, bf16[576,512]{1,0:T(8,128)(2,1)S(1)} %copy-done.10, pred[]{:T(512)S(6)} %eq.18), kind=kOutput, calls=%fused_computation.17 | convolution fusion | flops 1062789120 | bytes 4046849 | tf_op jit(solution)/shard_map/dot_general | solution.py:14
  148.7 1.2 copy.38
  149.9 5.6 %all-to-all-start.2 = ((bf16[36,16,896]{2,0,1:T(8,128)(2,1)}), bf16[36,16,896]{2,0,1:T(8,128)(2,1)S(1)}, u32[]{:S(2)}, u32[]{:S(2)}) async-start(bf16[36,16,896]{2,0,1:T(8,128)(2,1)} %copy.38), calls=%async_computation.2 | async-start | bytes 2293760 | tf_op jit(solution)/shard_map/all_to_all | solution.py:125
  155.5 3.7 %convolution_convert_fusion.4 = bf16[576,896]{1,0:T(8,128)(2,1)S(1)} fusion(bf16[896,1024]{1,0:T(8,128)(2,1)} %all-gather.3.cloned.1.call-done, bf16[576,512]{1,0:T(8,128)(2,1)} %copy-done.6, bf16[576,512]{1,0:T(8,128)(2,1)} %copy-done.8, pred[]{:T(512)S(6)} %eq.18), kind=kOutput, calls=%fused_computation.16 | convolution fusion | flops 1062789120 | bytes 4046849 | tf_op jit(solution)/shard_map/dot_general | solution.py:14
  159.2 1.2 copy.40
  160.4 19.7 %all-to-all-done.2 = bf16[36,16,896]{2,0,1:T(8,128)(2,1)S(1)} async-done(((bf16[36,16,896]{2,0,1:T(8,128)(2,1)}), bf16[36,16,896]{2,0,1:T(8,128)(2,1)S(1)}, u32[]{:S(2)}, u32[]{:S(2)}) %all-to-all-start.2) | async-done | bytes 1032224 | tf_op jit(solution)/shard_map/all_to_all | solution.py:125
  180.1 7.4 %all-to-all-start.3 = ((bf16[36,16,896]{2,0,1:T(8,128)(2,1)}), bf16[36,16,896]{2,0,1:T(8,128)(2,1)}, u32[]{:S(2)}, u32[]{:S(2)}) async-start(bf16[36,16,896]{2,0,1:T(8,128)(2,1)} %copy.40), calls=%async_computation.3 | async-start | bytes 2293760 | tf_op jit(solution)/shard_map/all_to_all | solution.py:87
  187.5 1.1 copy.39
  188.6 1.7 reshape.91
  190.3 21.8 %all-to-all-done.3 = bf16[36,16,896]{2,0,1:T(8,128)(2,1)} async-done(((bf16[36,16,896]{2,0,1:T(8,128)(2,1)}), bf16[36,16,896]{2,0,1:T(8,128)(2,1)}, u32[]{:S(2)}, u32[]{:S(2)}) %all-to-all-start.3) | async-done | bytes 1032224 | tf_op jit(solution)/shard_map/all_to_all | solution.py:87
  212.1 2.3 copy.41
  214.4 2.5 %reshape.93 = bf16[144,3584]{1,0:T(8,128)(2,1)} reshape(bf16[36,16,896]{2,1,0:T(8,128)(2,1)} %copy.41) | data formatting | bytes 2064384 | tf_op jit(solution)/shard_map/reshape | solution.py:126
  216.9 2.0 gather_fusion.3
  219.0 3.4 %gather_fusion.4 = bf16[128,3584]{1,0:T(8,128)(2,1)S(1)} fusion(bf16[144,3584]{1,0:T(8,128)(2,1)} %reshape.93, s32[1024]{0:T(1024)S(1)} %pad_clamp_fusion), kind=kCustom, calls=%fused_computation.4 | custom fusion | bytes 1835520 | tf_op jit(solution)/shard_map/gather | solution.py:128
  222.4 0.9 multiply_reduce_fusion
  223.2 3.7 %fusion.13 = (f32[448,1024]{1,0:T(8,128)}, f32[448,1024]{1,0:T(8,128)}) fusion(bf16[448,2048]{1,0:T(8,128)(2,1)} %reduce-scatter.2.cloned.1.call-done), kind=kLoop, calls=%fused_computation.61 | loop fusion | bytes 7340032 | tf_op jit(solution)/shard_map/slice | solution.py:124
  (42 shorter events, 0.9 us)
Async XLA Ops:
  7.2 2.8 %copy-start = (bf16[128,3584]{1,0:T(8,128)(2,1)S(1)}, bf16[128,3584]{1,0:T(8,128)(2,1)}, u32[]{:S(2)}) copy-start(bf16[128,3584]{1,0:T(8,128)(2,1)} %param.6) | copy-start | bytes 2752516
  15.4 8.2 %copy-start.2 = (bf16[128,3584]{1,0:T(8,128)(2,1)S(1)}, bf16[128,3584]{1,0:T(8,128)(2,1)}, u32[]{:S(2)}) copy-start(bf16[128,3584]{1,0:T(8,128)(2,1)} %param.7) | copy-start | bytes 2752516
  15.4 32.1 %all-to-all-start.1 = ((bf16[36,16,896]{2,0,1:T(8,128)(2,1)}), bf16[36,16,896]{2,0,1:T(8,128)(2,1)S(1)}, u32[]{:S(2)}, u32[]{:S(2)}) async-start(bf16[36,16,896]{2,0,1:T(8,128)(2,1)} %copy_select_fusion), calls=%async_computation.1 | async-start | bytes 2293760 | tf_op jit(solution)/shard_map/all_to_all | solution.py:60
  22.9 34.0 %all-gather.5.cloned.1.call-start = ((), (), s32[]{:S(2)}) async-start(), calls=%async_computation.6 | async-start | bytes 2752512 | tf_op jit(solution)/shard_map/all_gather | solution.py:36
  25.8 2.7 %copy-start.1 = (f32[128,1]{0,1:T(1,128)S(1)}, f32[128,1]{0,1:T(1,128)}, u32[]{:S(2)}) copy-start(f32[128,1]{0,1:T(1,128)} %param.8) | copy-start | bytes 1540
  47.4 32.0 %all-to-all-start = ((bf16[36,16,896]{2,0,1:T(8,128)(2,1)}), bf16[36,16,896]{2,0,1:T(8,128)(2,1)}, u32[]{:S(2)}, u32[]{:S(2)}) async-start(bf16[36,16,896]{2,0,1:T(8,128)(2,1)} %fusion.1), calls=%async_computation | async-start | bytes 2293760 | tf_op jit(solution)/shard_map/all_to_all | solution.py:88
  54.8 33.9 %all-gather.3.cloned.1.call-start = ((), (), s32[]{:S(2)}) async-start(), calls=%async_computation.5 | async-start | bytes 2752512 | tf_op jit(solution)/shard_map/all_gather | solution.py:37
  55.6 167.6 %reduce-scatter.2.cloned.1.call-start = ((), (), s32[]{:S(2)}) async-start(), calls=%async_computation.7 | async-start | bytes 5505024 | tf_op jit(solution)/shard_map/reduce_scatter | solution.py:116
  61.0 31.5 %collective-permute-start.2 = (bf16[1,576,512]{2,1,0:T(8,128)(2,1)}, bf16[1,576,512]{2,1,0:T(8,128)(2,1)}, u32[]{:S(2)}, u32[]{:S(2)}) collective-permute-start(bf16[1,576,512]{2,1,0:T(8,128)(2,1)} %get-tuple-element.13), channel_id=1, source_target_pairs={{0,1},{1,0},{2,3},{3,2},{4,5},{5,4},{6,7},{7,6},{8,9},{9,8},{10,11... | collective-permute-start | bytes 1769480 | tf_op jit(solution)/shard_map/ppermute | solution.py:10
  80.8 7.9 %copy-start.4 = (bf16[36,16,896]{2,1,0:T(8,128)(2,1)}, bf16[36,16,896]{2,1,0:T(8,128)(2,1)S(1)}, u32[]{:S(2)}) copy-start(bf16[36,16,896]{2,1,0:T(8,128)(2,1)S(1)} %copy.35) | copy-start | bytes 3096580
  92.5 2.9 %collective-permute-start = (bf16[1,576,512]{2,1,0:T(8,128)(2,1)}, bf16[1,576,512]{2,1,0:T(8,128)(2,1)}, u32[]{:S(2)}, u32[]{:S(2)}) collective-permute-start(bf16[1,576,512]{2,1,0:T(8,128)(2,1)} %get-tuple-element.9), channel_id=1, source_target_pairs={{0,1},{1,0},{2,3},{3,2},{4,5},{5,4},{6,7},{7,6},{8,9},{9,8},{10,11... | collective-permute-start | bytes 1769480 | tf_op jit(solution)/shard_map/ppermute | solution.py:10
  93.9 16.2 %collective-permute-start.3 = (bf16[2,576,256]{2,1,0:T(8,128)(2,1)S(1)}, bf16[2,576,256]{2,1,0:T(8,128)(2,1)S(1)}, u32[]{:S(2)}, u32[]{:S(2)}) collective-permute-start(bf16[2,576,256]{2,1,0:T(8,128)(2,1)S(1)} %get-tuple-element.11), channel_id=1, source_target_pairs={{0,2},{1,3},{2,0},{3,1},{4,6},{5,7},{6,4},{7,5},{8,10},{9,11},{10,... | collective-permute-start | bytes 1769480 | tf_op jit(solution)/shard_map/ppermute | solution.py:10
  96.8 25.5 %collective-permute-start.1 = (bf16[2,576,256]{2,1,0:T(8,128)(2,1)S(1)}, bf16[2,576,256]{2,1,0:T(8,128)(2,1)S(1)}, u32[]{:S(2)}, u32[]{:S(2)}) collective-permute-start(bf16[2,576,256]{2,1,0:T(8,128)(2,1)S(1)} %get-tuple-element.7), channel_id=1, source_target_pairs={{0,2},{1,3},{2,0},{3,1},{4,6},{5,7},{6,4},{7,5},{8,10},{9,11},{10,... | collective-permute-start | bytes 1769480 | tf_op jit(solution)/shard_map/ppermute | solution.py:10
  122.8 10.0 %collective-permute-start.6 = (bf16[576,256]{1,0:T(8,128)(2,1)S(1)}, bf16[576,256]{1,0:T(8,128)(2,1)S(1)}, u32[]{:S(2)}, u32[]{:S(2)}) collective-permute-start(bf16[576,256]{1,0:T(8,128)(2,1)S(1)} %get-tuple-element.14), channel_id=1, source_target_pairs={{0,2},{1,3},{2,0},{3,1},{4,6},{5,7},{6,4},{7,5},{8,10},{9,11},{10,... | collective-permute-start | bytes 884744 | tf_op jit(solution)/shard_map/ppermute | solution.py:10
  124.4 13.8 %copy-start.5 = (bf16[36,16,896]{2,1,0:T(8,128)(2,1)S(1)}, bf16[36,16,896]{2,1,0:T(8,128)(2,1)}, u32[]{:S(2)}) copy-start(bf16[36,16,896]{2,1,0:T(8,128)(2,1)} %copy-done.4) | copy-start | bytes 3096580
  124.4 13.5 %collective-permute-start.4 = (bf16[576,256]{1,0:T(8,128)(2,1)S(1)}, bf16[576,256]{1,0:T(8,128)(2,1)S(1)}, u32[]{:S(2)}, u32[]{:S(2)}) collective-permute-start(bf16[576,256]{1,0:T(8,128)(2,1)S(1)} %get-tuple-element.15), channel_id=1, source_target_pairs={{0,2},{1,3},{2,0},{3,1},{4,6},{5,7},{6,4},{7,5},{8,10},{9,11},{10,... | collective-permute-start | bytes 884744 | tf_op jit(solution)/shard_map/ppermute | solution.py:10
  133.0 6.8 %copy-start.6 = (bf16[576,512]{1,0:T(8,128)(2,1)}, bf16[576,512]{1,0:T(8,128)(2,1)S(1)}, u32[]{:S(2)}) copy-start(bf16[576,512]{1,0:T(8,128)(2,1)S(1)} %maximum_select_fusion.3) | copy-start | bytes 1769476
  133.0 5.1 %collective-permute-start.7 = (bf16[576,512]{1,0:T(8,128)(2,1)S(1)}, bf16[576,512]{1,0:T(8,128)(2,1)S(1)}, u32[]{:S(2)}, u32[]{:S(2)}) collective-permute-start(bf16[576,512]{1,0:T(8,128)(2,1)S(1)} %maximum_select_fusion.3), channel_id=1, source_target_pairs={{0,1},{1,0},{2,3},{3,2},{4,5},{5,4},{6,7},{7,6},{8,9},{9,8},{10,11... | collective-permute-start | bytes 1769480 | tf_op jit(solution)/shard_map/ppermute | solution.py:10
  138.0 2.9 %copy-start.3 = (bf16[36,16,896]{2,1,0:T(8,128)(2,1)S(1)}, bf16[36,16,896]{2,1,0:T(8,128)(2,1)}, u32[]{:S(2)}) copy-start(bf16[36,16,896]{2,1,0:T(8,128)(2,1)} %copy.37) | copy-start | bytes 3096580
  138.0 2.1 collective-permute-start.5
  138.1 1.7 copy-start.8
  140.1 0.8 copy-start.9
  144.7 1.1 copy-start.10
  149.9 30.2 %all-to-all-start.2 = ((bf16[36,16,896]{2,0,1:T(8,128)(2,1)}), bf16[36,16,896]{2,0,1:T(8,128)(2,1)S(1)}, u32[]{:S(2)}, u32[]{:S(2)}) async-start(bf16[36,16,896]{2,0,1:T(8,128)(2,1)} %copy.38), calls=%async_computation.2 | async-start | bytes 2293760 | tf_op jit(solution)/shard_map/all_to_all | solution.py:125
  160.4 27.1 %copy-start.7 = (s32[128,1]{0,1:T(1,128)S(1)}, s32[128,1]{0,1:T(1,128)}, u32[]{:S(2)}) copy-start(s32[128,1]{0,1:T(1,128)} %param.9) | copy-start | bytes 1540
  180.1 32.0 %all-to-all-start.3 = ((bf16[36,16,896]{2,0,1:T(8,128)(2,1)}), bf16[36,16,896]{2,0,1:T(8,128)(2,1)}, u32[]{:S(2)}, u32[]{:S(2)}) async-start(bf16[36,16,896]{2,0,1:T(8,128)(2,1)} %copy.40), calls=%async_computation.3 | async-start | bytes 2293760 | tf_op jit(solution)/shard_map/all_to_all | solution.py:87
Sparse Core Ops, SparseCore 0:
  25.3 31.5 all-gather.4
  58.4 30.3 all-gather.2
  144.9 49.0 reduce-scatter.1
where the time goes:
time: 236 us; the launch traced here: 233 us
  waiting for transfers between devices  120 us (51%)
  local copies, waits for them, and re-layouts  34.2 us (14%)
  starting transfers between devices  33.3 us (14%)
  matrix products  16 us (7%)
  other arithmetic  15.8 us (7%)
  between operations  14.1 us (6%)
    ppermute x8, waiting for transfers between devices, swapped(): lax.ppermute(x, axis, [(i, i ^ 1 << distance) for i in range(lax.axis_siz...  37.4 us
    all_to_all x1, waiting for transfers between devices, shards(): lax.all_to_all(out_buf, 'exp', split_axis=1, concat_axis=1, tiled=True)  21.8 us
    all_to_all x1, waiting for transfers between devices, shards(): lax.all_to_all(dx_buf, 'exp', split_axis=1, concat_axis=1, tiled=True)  19.7 us
    all_to_all x1, waiting for transfers between devices, shards(): lax.all_to_all(grads_buf, 'exp', split_axis=1, concat_axis=1, tiled=True)  18.1 us
    all_to_all x1, waiting for transfers between devices, shards(): lax.all_to_all(inputs_buf, 'exp', split_axis=1, concat_axis=1, tiled=True)  13.9 us
    all_gather x1, waiting for transfers between devices, shards(): lax.all_gather(w_down_t, 'rep', axis=0, tiled=True)  7.88 us
    all_to_all x1, starting transfers between devices, shards(): lax.all_to_all(inputs_buf, 'exp', split_axis=1, concat_axis=1, tiled=True)  7.49 us
    all_to_all x1, starting transfers between devices, shards(): lax.all_to_all(out_buf, 'exp', split_axis=1, concat_axis=1, tiled=True)  7.41 us
  transfers between devices with their start and end apart: 15, of which 10 were waited for; matrix products, arithmetic and copies ran while one was open for 21% of the time, Pallas kernels for 0%

commit v1 on v0

--- a/solution.py
+++ b/solution.py
@@ -82,9 +82,6 @@
             jnp.concatenate([partner_cols, hidden_act], axis=1),
             jnp.concatenate([hidden_act, partner_cols], axis=1),
         )
-    out_rows = contract_last(hidden_act, down_rows).astype(jnp.bfloat16)
-    out_buf = out_rows.reshape(capacity, n_devices, piece_width)
-    out_back = lax.all_to_all(out_buf, "exp", split_axis=1, concat_axis=1, tiled=True)
     grads_in = lax.all_to_all(grads_buf, "exp", split_axis=1, concat_axis=1, tiled=True)
     d_rows = grads_in.reshape(slot_rows, piece_width)
     grad_partial = jnp.dot(d_rows, down_rows, preferred_element_type=jnp.float32).astype(
@@ -100,6 +97,11 @@
         given_half = jnp.where(upper_side, lower_half, upper_half)
         grad_stack = jnp.concatenate([kept_half, swapped(given_half, "exp", bit_number)], axis=0)
     grad_cols = jnp.sum(grad_stack.astype(jnp.float32), axis=0)
+    gate_part = jnp.sum(grad_cols * (activation * gating), axis=1)
+    gate_back = lax.all_to_all(
+        gate_part.reshape(capacity, n_devices), "exp", split_axis=1, concat_axis=1, tiled=True
+    )
+    gate_table = jnp.sum(gate_back.reshape(capacity * experts, SLICES), axis=1)
     act_grad = (grad_cols * gating * (1.0 + activation * (1.0 - gating))).astype(jnp.bfloat16)
     for bit_number in reversed(range(slice_bits)):
         upper_side = exp_index >> bit_number & 1 == 1
@@ -113,21 +115,15 @@
     dx_buf = dx_rows.reshape(capacity, n_devices, piece_width)
     up_term = contract_first(x_rows, act_grad)
     down_term = contract_first(d_rows, hidden_act)
-    weight_sums = lax.psum_scatter(
-        jnp.concatenate([up_term, down_term], axis=1).astype(jnp.bfloat16),
-        "rep",
-        scatter_dimension=0,
-        tiled=True,
+    grad_down_t = lax.psum_scatter(
+        down_term.astype(jnp.bfloat16), "rep", scatter_dimension=0, tiled=True
     ).astype(jnp.float32)
-    hidden = up_rows.shape[1]
-    grad_up = weight_sums[:, :hidden]
-    grad_down_t = weight_sums[:, hidden:]
+    grad_up = lax.psum_scatter(
+        up_term.astype(jnp.bfloat16), "rep", scatter_dimension=0, tiled=True
+    ).astype(jnp.float32)
     dx_back = lax.all_to_all(dx_buf, "exp", split_axis=1, concat_axis=1, tiled=True)
-    out_table = out_back.reshape(capacity * experts, model_width)
     dx_table = dx_back.reshape(capacity * experts, model_width)
-    picked = out_table[position].astype(jnp.float32)
-    repeated = jnp.repeat(cotangent, top_count, axis=0).astype(jnp.float32)
-    grad_gates = jnp.sum(repeated * picked, axis=1).reshape(tok_dev, top_count)
+    grad_gates = gate_table[position].reshape(tok_dev, top_count) / gates
     grad_tokens = jnp.sum(
         dx_table[position].astype(jnp.float32).reshape(tok_dev, top_count, model_width), axis=1
     )

time: 236 us -> 213 us (0.903)
  local copies, waits for them, and re-layouts: 34.2 us -> 19.1 us
  waiting for transfers between devices: 120 us -> 115 us
  starting transfers between devices: 33.3 us -> 30.4 us
    all_to_all x1, waiting for transfers between devices: 21.8 us -> 2.25 us  [shards(): lax.all_to_all(gate_part.reshape(capacity, n_devices), 'exp', split_axis=...]
    all_gather x1, waiting for transfers between devices: 0.01 us -> 6.94 us  [shards(): lax.all_gather(w_up, 'rep', axis=0, tiled=True)]
    all_gather x1, waiting for transfers between devices: 7.88 us -> 1.04 us  [shards(): lax.all_gather(w_down_t, 'rep', axis=0, tiled=True)]
    ppermute x8, waiting for transfers between devices: 37.4 us -> 43.1 us  [swapped(): lax.ppermute(x, axis, [(i, i ^ 1 << distance) for i in range(lax.axis_siz...]
    all_to_all x1, waiting for transfers between devices: 13.9 us -> 18.8 us  [shards(): lax.all_to_all(inputs_buf, 'exp', split_axis=1, concat_axis=1, tiled=True)]
    convert_element_type x1 -> x2, other arithmetic: 0.28 us -> 5.23 us  [the longest x1 2.61 us: shards(): grad_up = lax.psum_scatter(up_term.astype(jnp.bfloat16), 'rep', scatter_d...]
    slice x1 -> x0, local copies, waits for them, and re-layouts: 3.7 us -> none  [shards(): grad_down_t = weight_sums[:, hidden:]]
    dot_general x2 -> x1, matrix products: 6.58 us -> 2.94 us  [contract_last(): lax.dot_general(left_side, right_side, (((1,), (1,)), ((), ())), preferre...]
  transfers between devices with their start and end apart: 15 -> 16, of which waited for: 10 -> 12; matrix products, arithmetic and copies ran while one was open for 21% -> 16% of each run, Pallas kernels for 0% -> 0%
where the time goes in v1:
time: 213 us; the launch traced here: 210 us
  waiting for transfers between devices  115 us (54%)
  starting transfers between devices  30.4 us (14%)
  local copies, waits for them, and re-layouts  19.1 us (9%)
  other arithmetic  17.2 us (8%)
  matrix products  14.9 us (7%)
  between operations  14.1 us (7%)
    ppermute x8, waiting for transfers between devices, swapped(): lax.ppermute(x, axis, [(i, i ^ 1 << distance) for i in range(lax.axis_siz...  43.1 us
    all_to_all x1, waiting for transfers between devices, shards(): lax.all_to_all(dx_buf, 'exp', split_axis=1, concat_axis=1, tiled=True)  22.4 us
    all_to_all x1, waiting for transfers between devices, shards(): lax.all_to_all(inputs_buf, 'exp', split_axis=1, concat_axis=1, tiled=True)  18.8 us
    all_to_all x1, waiting for transfers between devices, shards(): lax.all_to_all(grads_buf, 'exp', split_axis=1, concat_axis=1, tiled=True)  18.6 us
    all_to_all x1, starting transfers between devices, shards(): lax.all_to_all(grads_buf, 'exp', split_axis=1, concat_axis=1, tiled=True)  7.49 us
    all_to_all x1, starting transfers between devices, shards(): lax.all_to_all(inputs_buf, 'exp', split_axis=1, concat_axis=1, tiled=True)  7.4 us
    all_gather x1, waiting for transfers between devices, shards(): lax.all_gather(w_up, 'rep', axis=0, tiled=True)  6.94 us
    dot_general x2, matrix products, contract_first(): lax.dot_general(left_side, right_side, (((0,), (0,)), ((), ())), preferre...  5.79 us
  transfers between devices with their start and end apart: 16, of which 12 were waited for; matrix products, arithmetic and copies ran while one was open for 16% of the time, Pallas kernels for 0%

profile of v1, /device:TPU:0, one launch (start us, length us, event | category | flops | bytes accessed | tf_op | source)
XLA Modules:
  0.0 210.3 jit_solution(8214697811662068326)
XLA Ops:
  7.2 0.8 fusion.15
  8.0 0.2 reduce_window_sum.11
  8.2 0.8 select_reduce_fusion.1
  9.0 0.7 multiply_add_fusion
  9.7 0.1 select_reduce_fusion
  9.8 0.1 fusion.14
  9.9 2.2 %gather_fusion.1 = bf16[144,3584]{1,0:T(8,128)(2,1)} fusion(bf16[128,3584]{1,0:T(8,128)(2,1)S(1)} %copy-done, s32[1024]{0:T(1024)S(1)} %pad_clamp_fusion.1), kind=kCustom, calls=%fused_computation.1 | custom fusion | bytes 2064960 | tf_op jit(solution)/shard_map/gather | solution.py:57
  12.1 1.7 reshape.96
  13.8 1.6 gather_fusion
  15.5 0.1 broadcast_in_dim.58
  15.8 1.7 fusion.1
  17.5 7.5 %all-to-all-start = ((bf16[36,16,896]{2,0,1:T(8,128)(2,1)}), bf16[36,16,896]{2,0,1:T(8,128)(2,1)S(1)}, u32[]{:S(2)}, u32[]{:S(2)}) async-start(bf16[36,16,896]{2,0,1:T(8,128)(2,1)} %fusion.1), calls=%async_computation | async-start | bytes 2293760 | tf_op jit(solution)/shard_map/all_to_all | solution.py:85
  25.1 0.7 all-gather.3.cloned.1.call-update
  25.8 2.2 %gather_fusion.2 = bf16[144,3584]{1,0:T(8,128)(2,1)} fusion(bf16[128,3584]{1,0:T(8,128)(2,1)S(1)} %copy-done.2, s32[1024]{0:T(1024)S(1)} %pad_clamp_fusion.1), kind=kCustom, calls=%fused_computation.2 | custom fusion | bytes 2064960 | tf_op jit(solution)/shard_map/gather | solution.py:54
  27.9 1.7 gather.20
  29.7 1.3 copy_select_fusion
  31.0 18.6 %all-to-all-done = bf16[36,16,896]{2,0,1:T(8,128)(2,1)S(1)} async-done(((bf16[36,16,896]{2,0,1:T(8,128)(2,1)}), bf16[36,16,896]{2,0,1:T(8,128)(2,1)S(1)}, u32[]{:S(2)}, u32[]{:S(2)}) %all-to-all-start) | async-done | bytes 1032224 | tf_op jit(solution)/shard_map/all_to_all | solution.py:85
  49.6 7.4 %all-to-all-start.1 = ((bf16[36,16,896]{2,0,1:T(8,128)(2,1)}), bf16[36,16,896]{2,0,1:T(8,128)(2,1)}, u32[]{:S(2)}, u32[]{:S(2)}) async-start(bf16[36,16,896]{2,0,1:T(8,128)(2,1)} %copy_select_fusion), calls=%async_computation.1 | async-start | bytes 2293760 | tf_op jit(solution)/shard_map/all_to_all | solution.py:60
  57.0 0.7 all-gather.5.cloned.1.call-update
  57.8 0.1 copy.35
  57.9 1.0 all-gather.3.cloned.1.call-done
  59.0 2.9 %fusion.2 = bf16[1,576,1024]{2,1,0:T(8,128)(2,1)S(1)} fusion(bf16[576,896]{1,0:T(8,128)(2,1)S(1)} %bitcast.32, bf16[896,1024]{1,0:T(8,128)(2,1)} %all-gather.3.cloned.1.call-done), kind=kOutput, calls=%fused_computation.15 | convolution fusion | flops 1057554432 | bytes 4046848 | tf_op jit(solution)/shard_map/dot_general | solution.py:87
  61.9 0.9 broadcast_select_fusion.3
  62.8 18.8 %all-to-all-done.1 = bf16[36,16,896]{2,0,1:T(8,128)(2,1)} async-done(((bf16[36,16,896]{2,0,1:T(8,128)(2,1)}), bf16[36,16,896]{2,0,1:T(8,128)(2,1)}, u32[]{:S(2)}, u32[]{:S(2)}) %all-to-all-start.1) | async-done | bytes 1032224 | tf_op jit(solution)/shard_map/all_to_all | solution.py:60
  81.6 2.3 %copy.37 = bf16[36,16,896]{2,1,0:T(8,128)(2,1)} copy(bf16[36,16,896]{2,0,1:T(8,128)(2,1)} %all-to-all-done.1) | data formatting | bytes 2064384 | tf_op jit(solution)/shard_map/all_to_all | solution.py:60
  83.9 6.9 %all-gather.5.cloned.1.call-done = bf16[896,1024]{1,0:T(8,128)(2,1)} async-done(((bf16[448,1024]{1,0:T(8,128)(2,1)}), bf16[896,1024]{1,0:T(8,128)(2,1)}) %all-gather.5.cloned.1.call-update) | async-done | bytes 1835024 | tf_op jit(solution)/shard_map/all_gather | solution.py:36
  90.9 3.2 %fusion.3 = bf16[1,576,1024]{2,1,0:T(8,128)(2,1)S(1)} fusion(bf16[576,896]{1,0:T(8,128)(2,1)} %bitcast.34, bf16[896,1024]{1,0:T(8,128)(2,1)} %all-gather.5.cloned.1.call-done), kind=kOutput, calls=%fused_computation.16 | convolution fusion | flops 1057554432 | bytes 4046848 | tf_op jit(solution)/shard_map/dot_general | solution.py:62
  94.1 0.9 broadcast_select_fusion.1
  95.0 1.4 broadcast_select_fusion.7
  96.4 1.5 collective-permute-start.1
  97.9 1.4 broadcast_select_fusion.5
  99.3 1.0 collective-permute-start.3
  100.3 12.3 %collective-permute-done.1 = bf16[2,576,256]{2,1,0:T(8,128)(2,1)S(1)} collective-permute-done((bf16[2,576,256]{2,1,0:T(8,128)(2,1)S(1)}, bf16[2,576,256]{2,1,0:T(8,128)(2,1)S(1)}, u32[]{:S(2)}, u32[]{:S(2)}) %collective-permute-start.1) | collective-permute-done | bytes 589856 | tf_op jit(solution)/shard_map/ppermute | solution.py:10
  112.6 0.2 convert_reduce_fusion.1
  112.8 12.1 %collective-permute-done.3 = bf16[2,576,256]{2,1,0:T(8,128)(2,1)S(1)} collective-permute-done((bf16[2,576,256]{2,1,0:T(8,128)(2,1)S(1)}, bf16[2,576,256]{2,1,0:T(8,128)(2,1)S(1)}, u32[]{:S(2)}, u32[]{:S(2)}) %collective-permute-start.3) | collective-permute-done | bytes 589856 | tf_op jit(solution)/shard_map/ppermute | solution.py:10
  124.8 0.2 convert_reduce_fusion
  125.0 0.4 multiply_reduce_fusion
  125.4 1.5 collective-permute-start.4
  127.0 7.2 %collective-permute-done.4 = bf16[576,256]{1,0:T(8,128)(2,1)S(1)} collective-permute-done((bf16[576,256]{1,0:T(8,128)(2,1)S(1)}, bf16[576,256]{1,0:T(8,128)(2,1)S(1)}, u32[]{:S(2)}, u32[]{:S(2)}) %collective-permute-start.4) | collective-permute-done | bytes 294944 | tf_op jit(solution)/shard_map/ppermute | solution.py:10
  134.1 0.1 maximum_select_fusion.3
  134.4 2.0 collective-permute-done.5
  136.3 0.8 copy-done.5
  137.2 2.9 %convolution_convert_fusion.1 = bf16[896,1024]{1,0:T(8,128)(2,1)} fusion(bf16[576,896]{1,0:T(8,128)(2,1)S(1)} %bitcast.35, bf16[576,512]{1,0:T(8,128)(2,1)S(1)} %maximum_select_fusion.3, bf16[576,512]{1,0:T(8,128)(2,1)S(1)} %collective-permute-done.5, pred[]{:T(512)S(6)} %eq.18), kind=kOutput, calls=%fused_computation.11 | convolution fusion | flops 1063190528 | bytes 4046849 | tf_op jit(solution)/shard_map/dot_general | solution.py:20
  140.1 0.2 reduce-scatter.5.cloned.1.call-start
  140.3 1.5 collective-permute-start.6
  141.8 7.6 %collective-permute-done.6 = bf16[576,256]{1,0:T(8,128)(2,1)S(1)} collective-permute-done((bf16[576,256]{1,0:T(8,128)(2,1)S(1)}, bf16[576,256]{1,0:T(8,128)(2,1)S(1)}, u32[]{:S(2)}, u32[]{:S(2)}) %collective-permute-start.6) | collective-permute-done | bytes 294944 | tf_op jit(solution)/shard_map/ppermute | solution.py:10
  149.4 0.1 maximum_select_fusion.4
  149.6 2.0 collective-permute-done.7
  151.6 2.9 %convolution_convert_fusion = bf16[896,1024]{1,0:T(8,128)(2,1)} fusion(bf16[576,896]{1,0:T(8,128)(2,1)S(1)} %bitcast.33, bf16[576,512]{1,0:T(8,128)(2,1)S(1)} %maximum_select_fusion.4, bf16[576,512]{1,0:T(8,128)(2,1)S(1)} %collective-permute-done.7, pred[]{:T(512)S(6)} %eq.18), kind=kOutput, calls=%fused_computation.10 | convolution fusion | flops 1063190528 | bytes 4046849 | tf_op jit(solution)/shard_map/dot_general | solution.py:20
  154.6 0.7 copy.40
  155.3 5.6 %all-to-all-start.3 = ((f32[36,16,1]{0,2,1:T(1,128)}), f32[36,16,1]{0,2,1:T(1,128)S(1)}, u32[]{:S(2)}, u32[]{:S(2)}) async-start(f32[36,16,1]{0,2,1:T(1,128)} %copy.40), calls=%async_computation.3 | async-start | bytes 16384 | tf_op jit(solution)/shard_map/all_to_all | solution.py:101
  160.9 2.9 %convolution_convert_fusion.4 = bf16[576,896]{1,0:T(8,128)(2,1)S(1)} fusion(bf16[896,1024]{1,0:T(8,128)(2,1)} %all-gather.5.cloned.1.call-done, bf16[576,512]{1,0:T(8,128)(2,1)S(1)} %maximum_select_fusion.3, bf16[576,512]{1,0:T(8,128)(2,1)S(1)} %copy-done.6, pred[]{:T(512)S(6)} %eq.18), kind=kOutput, calls=%fused_computation.14 | convolution fusion | flops 1062789120 | bytes 4046849 | tf_op jit(solution)/shard_map/dot_general | solution.py:14
  163.9 1.2 copy.38
  165.1 2.2 %all-to-all-done.3 = f32[36,16,1]{0,2,1:T(1,128)S(1)} async-done(((f32[36,16,1]{0,2,1:T(1,128)}), f32[36,16,1]{0,2,1:T(1,128)S(1)}, u32[]{:S(2)}, u32[]{:S(2)}) %all-to-all-start.3) | async-done | bytes 2336 | tf_op jit(solution)/shard_map/all_to_all | solution.py:101
  167.3 3.9 %all-to-all-start.2 = ((bf16[36,16,896]{2,0,1:T(8,128)(2,1)}), bf16[36,16,896]{2,0,1:T(8,128)(2,1)S(1)}, u32[]{:S(2)}, u32[]{:S(2)}) async-start(bf16[36,16,896]{2,0,1:T(8,128)(2,1)} %copy.38), calls=%async_computation.2 | async-start | bytes 2293760 | tf_op jit(solution)/shard_map/all_to_all | solution.py:124
  171.4 0.1 reduce_sum.66
  171.6 1.3 gather_fusion.4
  172.8 0.5 bitcast_divide_fusion
  173.4 22.4 %all-to-all-done.2 = bf16[36,16,896]{2,0,1:T(8,128)(2,1)S(1)} async-done(((bf16[36,16,896]{2,0,1:T(8,128)(2,1)}), bf16[36,16,896]{2,0,1:T(8,128)(2,1)S(1)}, u32[]{:S(2)}, u32[]{:S(2)}) %all-to-all-start.2) | async-done | bytes 1032224 | tf_op jit(solution)/shard_map/all_to_all | solution.py:124
  195.8 0.1 copy.39
  195.9 0.6 reshape.93
  196.5 2.0 gather_fusion.3
  198.6 2.6 %convert_element_type.62 = f32[448,1024]{1,0:T(8,128)} convert(bf16[448,1024]{1,0:T(8,128)(2,1)} %reduce-scatter.3.cloned.1.call-done) | non-fusion elementwise | flops 458752 | bytes 2752512 | tf_op jit(solution)/shard_map/convert_element_type | solution.py:123
  201.2 2.6 %convert_element_type.65 = f32[448,1024]{1,0:T(8,128)} convert(bf16[448,1024]{1,0:T(8,128)(2,1)} %reduce-scatter.5.cloned.1.call-done) | non-fusion elementwise | flops 458752 | bytes 2752512 | tf_op jit(solution)/shard_map/convert_element_type | solution.py:120
  (38 shorter events, 0.9 us)
Async XLA Ops:
  7.2 2.8 %copy-start = (bf16[128,3584]{1,0:T(8,128)(2,1)S(1)}, bf16[128,3584]{1,0:T(8,128)(2,1)}, u32[]{:S(2)}) copy-start(bf16[128,3584]{1,0:T(8,128)(2,1)} %param.7) | copy-start | bytes 2752516
  12.1 1.7 copy-start.1
  17.5 8.2 %copy-start.2 = (bf16[128,3584]{1,0:T(8,128)(2,1)S(1)}, bf16[128,3584]{1,0:T(8,128)(2,1)}, u32[]{:S(2)}) copy-start(bf16[128,3584]{1,0:T(8,128)(2,1)} %param.6) | copy-start | bytes 2752516
  17.5 32.1 %all-to-all-start = ((bf16[36,16,896]{2,0,1:T(8,128)(2,1)}), bf16[36,16,896]{2,0,1:T(8,128)(2,1)S(1)}, u32[]{:S(2)}, u32[]{:S(2)}) async-start(bf16[36,16,896]{2,0,1:T(8,128)(2,1)} %fusion.1), calls=%async_computation | async-start | bytes 2293760 | tf_op jit(solution)/shard_map/all_to_all | solution.py:85
  25.0 33.9 %all-gather.3.cloned.1.call-start = ((), (), s32[]{:S(2)}) async-start(), calls=%async_computation.6 | async-start | bytes 2752512 | tf_op jit(solution)/shard_map/all_gather | solution.py:37
  49.6 32.0 %all-to-all-start.1 = ((bf16[36,16,896]{2,0,1:T(8,128)(2,1)}), bf16[36,16,896]{2,0,1:T(8,128)(2,1)}, u32[]{:S(2)}, u32[]{:S(2)}) async-start(bf16[36,16,896]{2,0,1:T(8,128)(2,1)} %copy_select_fusion), calls=%async_computation.1 | async-start | bytes 2293760 | tf_op jit(solution)/shard_map/all_to_all | solution.py:60
  57.0 33.9 %all-gather.5.cloned.1.call-start = ((), (), s32[]{:S(2)}) async-start(), calls=%async_computation.7 | async-start | bytes 2752512 | tf_op jit(solution)/shard_map/all_gather | solution.py:36
  57.7 140.8 %reduce-scatter.3.cloned.1.call-start = ((), (), s32[]{:S(2)}) async-start(), calls=%async_computation.8 | async-start | bytes 2752512 | tf_op jit(solution)/shard_map/reduce_scatter | solution.py:121
  62.8 32.2 %collective-permute-start = (bf16[1,576,512]{2,1,0:T(8,128)(2,1)}, bf16[1,576,512]{2,1,0:T(8,128)(2,1)}, u32[]{:S(2)}, u32[]{:S(2)}) collective-permute-start(bf16[1,576,512]{2,1,0:T(8,128)(2,1)} %get-tuple-element.9), channel_id=1, source_target_pairs={{0,1},{1,0},{2,3},{3,2},{4,5},{5,4},{6,7},{7,6},{8,9},{9,8},{10,11... | collective-permute-start | bytes 1769480 | tf_op jit(solution)/shard_map/ppermute | solution.py:10
  95.0 2.9 %collective-permute-start.2 = (bf16[1,576,512]{2,1,0:T(8,128)(2,1)}, bf16[1,576,512]{2,1,0:T(8,128)(2,1)}, u32[]{:S(2)}, u32[]{:S(2)}) collective-permute-start(bf16[1,576,512]{2,1,0:T(8,128)(2,1)} %get-tuple-element.13), channel_id=1, source_target_pairs={{0,1},{1,0},{2,3},{3,2},{4,5},{5,4},{6,7},{7,6},{8,9},{9,8},{10,11... | collective-permute-start | bytes 1769480 | tf_op jit(solution)/shard_map/ppermute | solution.py:10
  96.4 16.2 %collective-permute-start.1 = (bf16[2,576,256]{2,1,0:T(8,128)(2,1)S(1)}, bf16[2,576,256]{2,1,0:T(8,128)(2,1)S(1)}, u32[]{:S(2)}, u32[]{:S(2)}) collective-permute-start(bf16[2,576,256]{2,1,0:T(8,128)(2,1)S(1)} %get-tuple-element.7), channel_id=1, source_target_pairs={{0,2},{1,3},{2,0},{3,1},{4,6},{5,7},{6,4},{7,5},{8,10},{9,11},{10,... | collective-permute-start | bytes 1769480 | tf_op jit(solution)/shard_map/ppermute | solution.py:10
  99.3 25.5 %collective-permute-start.3 = (bf16[2,576,256]{2,1,0:T(8,128)(2,1)S(1)}, bf16[2,576,256]{2,1,0:T(8,128)(2,1)S(1)}, u32[]{:S(2)}, u32[]{:S(2)}) collective-permute-start(bf16[2,576,256]{2,1,0:T(8,128)(2,1)S(1)} %get-tuple-element.11), channel_id=1, source_target_pairs={{0,2},{1,3},{2,0},{3,1},{4,6},{5,7},{6,4},{7,5},{8,10},{9,11},{10,... | collective-permute-start | bytes 1769480 | tf_op jit(solution)/shard_map/ppermute | solution.py:10
  125.0 12.1 %copy-start.3 = (bf16[36,16,896]{2,1,0:T(8,128)(2,1)S(1)}, bf16[36,16,896]{2,1,0:T(8,128)(2,1)}, u32[]{:S(2)}) copy-start(bf16[36,16,896]{2,1,0:T(8,128)(2,1)} %copy.37) | copy-start | bytes 3096580
  125.4 8.7 %collective-permute-start.4 = (bf16[576,256]{1,0:T(8,128)(2,1)S(1)}, bf16[576,256]{1,0:T(8,128)(2,1)S(1)}, u32[]{:S(2)}, u32[]{:S(2)}) collective-permute-start(bf16[576,256]{1,0:T(8,128)(2,1)S(1)} %get-tuple-element.5), channel_id=1, source_target_pairs={{0,2},{1,3},{2,0},{3,1},{4,6},{5,7},{6,4},{7,5},{8,10},{9,11},{10,... | collective-permute-start | bytes 884744 | tf_op jit(solution)/shard_map/ppermute | solution.py:10
  134.3 2.1 collective-permute-start.5
  136.3 0.8 copy-start.5
  140.1 61.1 %reduce-scatter.5.cloned.1.call-start = ((), (), s32[]{:S(2)}) async-start(), calls=%async_computation.9 | async-start | bytes 2752512 | tf_op jit(solution)/shard_map/reduce_scatter | solution.py:118
  140.3 9.1 %collective-permute-start.6 = (bf16[576,256]{1,0:T(8,128)(2,1)S(1)}, bf16[576,256]{1,0:T(8,128)(2,1)S(1)}, u32[]{:S(2)}, u32[]{:S(2)}) collective-permute-start(bf16[576,256]{1,0:T(8,128)(2,1)S(1)} %get-tuple-element.14), channel_id=1, source_target_pairs={{0,2},{1,3},{2,0},{3,1},{4,6},{5,7},{6,4},{7,5},{8,10},{9,11},{10,... | collective-permute-start | bytes 884744 | tf_op jit(solution)/shard_map/ppermute | solution.py:10
  149.6 2.1 collective-permute-start.7
  154.5 6.4 %copy-start.6 = (bf16[576,512]{1,0:T(8,128)(2,1)S(1)}, bf16[576,512]{1,0:T(8,128)(2,1)}, u32[]{:S(2)}) copy-start(bf16[576,512]{1,0:T(8,128)(2,1)} %copy-done.5) | copy-start | bytes 1769476
  155.3 12.0 %all-to-all-start.3 = ((f32[36,16,1]{0,2,1:T(1,128)}), f32[36,16,1]{0,2,1:T(1,128)S(1)}, u32[]{:S(2)}, u32[]{:S(2)}) async-start(f32[36,16,1]{0,2,1:T(1,128)} %copy.40), calls=%async_computation.3 | async-start | bytes 16384 | tf_op jit(solution)/shard_map/all_to_all | solution.py:101
  165.1 6.2 %copy-start.4 = (s32[128,1]{0,1:T(1,128)S(1)}, s32[128,1]{0,1:T(1,128)}, u32[]{:S(2)}) copy-start(s32[128,1]{0,1:T(1,128)} %param.9) | copy-start | bytes 1540
  167.3 28.5 %all-to-all-start.2 = ((bf16[36,16,896]{2,0,1:T(8,128)(2,1)}), bf16[36,16,896]{2,0,1:T(8,128)(2,1)S(1)}, u32[]{:S(2)}, u32[]{:S(2)}) async-start(bf16[36,16,896]{2,0,1:T(8,128)(2,1)} %copy.38), calls=%async_computation.2 | async-start | bytes 2293760 | tf_op jit(solution)/shard_map/all_to_all | solution.py:124
Sparse Core Ops, SparseCore 0:
  27.4 31.5 all-gather.2
  60.5 30.3 all-gather.4
  140.2 28.9 reduce-scatter.2
  171.4 28.9 reduce-scatter.4

commit v2 on v1

v2 whole, which is shorter than its diff:
```python
import functools

import jax
import jax.numpy as jnp
from jax import lax
from jax.experimental import pallas as pl
from jax.experimental.pallas import tpu as pltpu
from jax.sharding import PartitionSpec as P

SLICES = 4
MESH = pl.DeviceIdType.MESH
F32, BF16 = jnp.float32, jnp.bfloat16


def dot(left, right, dims, precision=None):
    return lax.dot_general(
        left, right, ((dims[:1], dims[1:]), ((), ())), preferred_element_type=F32, precision=precision
    )


def tiles(width, step=256):
    return [(start, min(step, width - start)) for start in range(0, width, step)]


def kernel(
    n_rep, planes, capacity, slots,
    tokens, cot, gates, routes, w_up, w_down,
    grad_tokens, gate_sums, weight_sums,
    out_grad, raw, place, weights, packed, rows, part, first, first_in, second_in,
    act, hidden, terms, dx, dx_in, gate_row, gate_in, back, gate_back, gate_mates,
    local_sem, raw_send, raw_recv, place_send, place_recv, weight_send, weight_recv,
    plane_send, plane_recv, a_send, a_recv, b_send, b_recv, c_send, c_recv, d_send, d_recv,
    dx_send, dx_recv, gate_send, gate_recv, term_send, term_recv, back_send, back_recv,
    mate_send, mate_recv,
):
    rep, me = lax.axis_index("rep"), lax.axis_index("exp")
    plane, q = me // SLICES, me % SLICES
    low, high = q % 2, q // 2
    tok_dev, width = tokens.shape[0], raw.shape[3]
    own_rows, hid = w_up.shape
    half, quarter = hid // 2, hid // 4
    items = 2 * planes

    def mate(distance):
        return (rep, plane * SLICES + (q + distance) % SLICES)

    def ahead(distance):
        return (rep, (plane + distance) % planes * SLICES + q)

    def behind(distance):
        return (rep, (plane + planes - distance) % planes * SLICES + q)

    def replica(distance):
        return ((rep + distance) % n_rep, me)

    near = (rep, plane * SLICES + high * 2 + 1 - low)
    far = (rep, plane * SLICES + (1 - high) * 2 + low)

    def copy(source, target, send_sem, recv_sem, device):
        return pltpu.make_async_remote_copy(
            src_ref=source, dst_ref=target, send_sem=send_sem, recv_sem=recv_sem,
            device_id=device, device_id_type=MESH,
        )

    def feature_block(index):
        return pl.ds(pl.multiple_of(index * width, 128), width)

    def weight_rows(index):
        return pl.ds(pl.multiple_of(index * own_rows, 16), own_rows)

    def raw_copy(a, j):
        source = (tokens, out_grad)[a]
        return copy(
            source.at[:, feature_block((q + j) % SLICES)], raw.at[a, q],
            raw_send.at[a, j], raw_recv.at[a, j], mate(j),
        )

    def place_copy(j):
        return copy(place.at[q], place.at[q], place_send.at[j], place_recv.at[j], mate(j))

    def weight_copy(a, d):
        source = (w_up, w_down)[a]
        return copy(
            source, weights.at[a, weight_rows(rep)],
            weight_send.at[a, d], weight_recv.at[a, d], replica(d),
        )

    def plane_copy(a, k):
        return copy(
            packed.at[a, k], rows.at[a, k], plane_send.at[a, k], plane_recv.at[a, k], ahead(k)
        )

    def a_copy(s):
        other = pl.ds(pl.multiple_of((1 - low) * half, 128), half)
        return copy(part.at[s, :, other], first_in.at[s], a_send.at[s], a_recv.at[s], near)

    def b_copy(s):
        other = pl.ds(pl.multiple_of((1 - high) * quarter, 128), quarter)
        return copy(first.at[s, :, other], second_in.at[s], b_send.at[s], b_recv.at[s], far)

    own_quarter = pl.ds(pl.multiple_of(low * half + high * quarter, 128), quarter)
    own_half = pl.ds(pl.multiple_of(low * half, 128), half)

    def c_copy(s):
        block = hidden.at[s, :, own_quarter]
        return copy(block, block, c_send.at[s], c_recv.at[s], far)

    def d_copy(s):
        block = hidden.at[s, :, own_half]
        return copy(block, block, d_send.at[s], d_recv.at[s], near)

    def dx_copy(k):
        return copy(dx.at[k], dx_in.at[k], dx_send.at[k], dx_recv.at[k], behind(k))

    def gate_copy(k):
        return copy(gate_row.at[k], gate_in.at[k], gate_send.at[k], gate_recv.at[k], behind(k))

    def term_copy(a, d):
        return copy(
            terms.at[a, weight_rows((rep + d) % n_rep)], weight_sums.at[a, d],
            term_send.at[a, d], term_recv.at[a, d], replica(d),
        )

    def back_copy(j):
        return copy(
            back.at[j], grad_tokens.at[:, feature_block(q)],
            back_send.at[j], back_recv.at[j], mate(j),
        )

    def mate_copy(j):
        return copy(gate_back.at[j], gate_mates.at[j], mate_send.at[j], mate_recv.at[j], mate(j))

    barrier = pltpu.get_barrier_semaphore()
    peers = [mate(j) for j in range(1, SLICES)] + [replica(d) for d in range(1, n_rep)]
    for device in peers:
        pl.semaphore_signal(barrier, inc=1, device_id=device, device_id_type=MESH)

    @pl.loop(1, planes)
    def _(k):
        pl.semaphore_signal(barrier, inc=1, device_id=ahead(k), device_id_type=MESH)

    pl.semaphore_wait(barrier, len(peers) + planes - 1)

    for j in range(1, SLICES):
        raw_copy(0, j).start()
    for d in range(1, n_rep):
        weight_copy(0, d).start()
    local = [
        pltpu.make_async_copy(tokens.at[:, feature_block(q)], raw.at[0, q], local_sem.at[0]),
        pltpu.make_async_copy(w_up, weights.at[0, weight_rows(rep)], local_sem.at[1]),
        pltpu.make_async_copy(w_down, weights.at[1, weight_rows(rep)], local_sem.at[2]),
    ]
    for c in local:
        c.start()

    route = routes[...]
    count = max(8, planes)
    onehot = (lax.broadcasted_iota(jnp.int32, (count, tok_dev), 0) == route).astype(F32)
    before = (
        lax.broadcasted_iota(jnp.int32, (tok_dev, tok_dev), 0)
        < lax.broadcasted_iota(jnp.int32, (tok_dev, tok_dev), 1)
    ).astype(F32)
    slot = jnp.sum(onehot * dot(onehot, before, (1, 0)), axis=0, keepdims=True)
    position = (route * slots + q * capacity).astype(F32) + slot
    place[q] = jnp.broadcast_to(position, (8, tok_dev))
    for j in range(1, SLICES):
        place_copy(j).start()

    gate = gates[...]
    for m in range(SLICES):
        block = slice(m * width, (m + 1) * width)
        out_grad[:, block] = (gate * cot[:, block].astype(F32)).astype(BF16)
    for j in range(1, SLICES):
        raw_copy(1, j).start()
    for d in range(1, n_rep):
        weight_copy(1, d).start()
    local_grad = pltpu.make_async_copy(
        out_grad.at[:, feature_block(q)], raw.at[1, q], local_sem.at[3]
    )
    local_grad.start()
    gate_row[...] = jnp.zeros_like(gate_row)

    for j in range(1, SLICES):
        place_copy(j).wait_recv()
    places = jnp.concatenate([place[m, 0:1, :] for m in range(SLICES)], axis=1)

    def chosen(expert, positions, kind):
        number = lax.broadcasted_iota(jnp.int32, (slots, positions.shape[1]), 0) + expert * slots
        return jnp.where(number.astype(F32) == positions, 1.0, 0.0).astype(kind)

    def pack(a, k, target):
        matrix = chosen((plane + k) % planes, places, BF16)
        for start, size in tiles(width):
            source = raw[a, :, :, start : start + size].reshape(SLICES * tok_dev, size)
            target[a, k, :, start : start + size] = dot(matrix, source, (1, 0)).astype(BF16)

    for a in range(2):
        for j in range(1, SLICES):
            sender = (q + SLICES - j) % SLICES
            copy(
                raw.at[a, sender], raw.at[a, sender], raw_send.at[a, j], raw_recv.at[a, j], mate(j)
            ).wait_recv()
        (local[0], local_grad)[a].wait()

        @pl.loop(1, planes)
        def _(k):
            pack(a, k, packed)
            plane_copy(a, k).start()

        pack(a, 0, rows)
    local[1].wait()
    local[2].wait()

    def weight_term(a):
        @pl.loop(0, width // 128)
        def _(i):
            features = pl.ds(pl.multiple_of(i * 128, 128), 128)
            left = rows[a, :, :, features].reshape(planes * slots, 128)
            for start, size in tiles(hid, 512):
                right = hidden[(1 - a) * planes : (2 - a) * planes, :, start : start + size]
                right = right.reshape(planes * slots, size)
                terms[a, features, start : start + size] = dot(left, right, (0, 0)).astype(BF16)

        for d in range(1, n_rep):
            term_copy(a, d).start()
        weight_sums[a, 0] = terms[a, weight_rows(rep), :]

    @pl.loop(0, items + 4)
    def _(s):
        @pl.when(s < items)
        def _():
            a, k = s // planes, s % planes

            @pl.when(k == 0)
            def _():
                for d in range(1, n_rep):
                    landed = weights.at[a, weight_rows((rep + n_rep - d) % n_rep)]
                    copy(
                        landed, landed, weight_send.at[a, d], weight_recv.at[a, d], replica(d)
                    ).wait_recv()

            @pl.when(k > 0)
            def _():
                plane_copy(a, k).wait_recv()

            left = rows[a, k]
            for start, size in tiles(hid):
                part[s, :, start : start + size] = dot(
                    left, weights[a, :, start : start + size], (1, 0)
                ).astype(BF16)
            a_copy(s).start()

        @pl.when(s >= 4)
        def _():
            t = s - 4
            landed = hidden.at[t, :, pl.ds(pl.multiple_of((1 - low) * half, 128), half)]
            copy(landed, landed, d_send.at[t], d_recv.at[t], near).wait_recv()

            @pl.when(t >= planes)
            def _():
                k = t - planes
                left = hidden[t]
                for start, size in tiles(width):
                    dx[k, :, start : start + size] = dot(
                        left, weights[0, start : start + size, :], (1, 1)
                    ).astype(BF16)

                @pl.when(k > 0)
                def _():
                    gate_copy(k).start()
                    dx_copy(k).start()

        @pl.when((s >= 3) & (s < items + 3))
        def _():
            t = s - 3
            landed = hidden.at[
                t, :, pl.ds(pl.multiple_of(low * half + (1 - high) * quarter, 128), quarter)
            ]
            copy(landed, landed, c_send.at[t], c_recv.at[t], far).wait_recv()
            d_copy(t).start()

        @pl.when((s >= 2) & (s < items + 2))
        def _():
            t = s - 2
            b_copy(t).wait_recv()
            mine = pl.ds(pl.multiple_of(high * quarter, 128), quarter)
            total = first[t, :, mine].astype(F32) + second_in[t].astype(F32)

            @pl.when(t < planes)
            def _():
                act[t] = total
                hidden[t, :, own_quarter] = (total * jax.nn.sigmoid(total)).astype(BF16)

            @pl.when(t >= planes)
            def _():
                k = t - planes
                value = act[k]
                gating = jax.nn.sigmoid(value)
                hidden[t, :, own_quarter] = (
                    total * gating * (1.0 + value * (1.0 - gating))
                ).astype(BF16)
                gate_row[k, :, 0:slots] = dot(
                    jnp.ones((8, quarter), F32), total * (value * gating), (1, 1),
                    lax.Precision.HIGHEST,
                )

            c_copy(t).start()

        @pl.when((s >= 1) & (s < items + 1))
        def _():
            t = s - 1
            a_copy(t).wait_recv()
            first[t] = (part[t, :, own_half].astype(F32) + first_in[t].astype(F32)).astype(BF16)
            b_copy(t).start()

        @pl.when(s == items)
        def _():
            weight_term(1)

    weight_term(0)

    @pl.loop(1, planes)
    def _(k):
        gate_copy(k).wait_recv()
        dx_copy(k).wait_recv()

    for j in (2, 1, 3, 0):
        positions = place[(q + j) % SLICES][0:1, :]
        blocks = [chosen((plane + k) % planes, positions, BF16) for k in range(planes)]
        matrix = jnp.concatenate(blocks, axis=0)
        for start, size in tiles(width):
            landed = jnp.concatenate(
                [dx[0, :, start : start + size]]
                + [dx_in[k, :, start : start + size] for k in range(1, planes)],
                axis=0,
            )
            back[j, :, start : start + size] = dot(matrix, landed, (0, 0)).astype(BF16)
        sums = jnp.zeros((8, tok_dev), F32)
        for k in range(planes):
            source = gate_row if k == 0 else gate_in
            sums += dot(
                source[k, :, 0:slots], blocks[k].astype(F32), (1, 0), lax.Precision.HIGHEST
            )
        gate_back[j] = sums
        if j > 0:
            back_copy(j).start()
            mate_copy(j).start()
    last = pltpu.make_async_copy(
        back.at[0], grad_tokens.at[:, feature_block(q)], local_sem.at[0]
    )
    last.start()
    total = gate_back[0]
    for j in range(1, SLICES):
        mate_copy(j).wait_recv()
        total += gate_mates[j]
    gate_sums[...] = total
    last.wait()
    for j in range(1, SLICES):
        landed = grad_tokens.at[:, feature_block((q + SLICES - j) % SLICES)]
        copy(landed, landed, back_send.at[j], back_recv.at[j], mate(j)).wait_recv()
    for a in range(2):
        for d in range(1, n_rep):
            term_copy(a, d).wait_recv()
            term_copy(a, d).wait_send()
            weight_copy(a, d).wait_send()
        for j in range(1, SLICES):
            raw_copy(a, j).wait_send()

        @pl.loop(1, planes)
        def _(k):
            plane_copy(a, k).wait_send()

    for j in range(1, SLICES):
        place_copy(j).wait_send()
        back_copy(j).wait_send()
        mate_copy(j).wait_send()

    @pl.loop(1, planes)
    def _(k):
        dx_copy(k).wait_send()
        gate_copy(k).wait_send()

    @pl.loop(0, items)
    def _(s):
        a_copy(s).wait_send()
        b_copy(s).wait_send()
        c_copy(s).wait_send()
        d_copy(s).wait_send()


def shards(tokens, cotangent, gates, routes, w_up, w_down_t):
    tok_dev, top_count = routes.shape
    model_width = tokens.shape[1]
    width = model_width // SLICES
    n_rep, n_exp = lax.axis_size("rep"), lax.axis_size("exp")
    planes = n_exp // SLICES
    capacity = min(tok_dev, max(2, 9 * tok_dev * top_count // (8 * planes)))
    slots = -(-SLICES * capacity // 16) * 16
    lanes = -(-slots // 128) * 128
    own_rows, hid = w_up.shape
    items = 2 * planes
    dma = pltpu.SemaphoreType.DMA
    vmem = pl.BlockSpec(memory_space=pltpu.VMEM)
    pairs = []
    for shape in (
        (2, SLICES), (SLICES,), (2, n_rep), (2, planes), (items,), (items,), (items,), (items,),
        (planes,), (planes,), (2, n_rep), (SLICES,), (SLICES,),
    ):
        pairs += [dma(shape), dma(shape)]
    grad_tokens, gate_sums, weight_sums = pl.pallas_call(
        functools.partial(kernel, n_rep, planes, capacity, slots),
        out_shape=(
            jax.ShapeDtypeStruct((tok_dev, model_width), BF16),
            jax.ShapeDtypeStruct((8, tok_dev), F32),
            jax.ShapeDtypeStruct((2, n_rep, own_rows, hid), BF16),
        ),
        in_specs=[vmem] * 6,
        out_specs=(vmem, vmem, vmem),
        scratch_shapes=[
            pltpu.VMEM((tok_dev, model_width), BF16),
            pltpu.VMEM((2, SLICES, tok_dev, width), BF16),
            pltpu.VMEM((SLICES, 8, tok_dev), F32),
            pltpu.VMEM((2, width, hid), BF16),
            pltpu.VMEM((2, planes, slots, width), BF16),
            pltpu.VMEM((2, planes, slots, width), BF16),
            pltpu.VMEM((items, slots, hid), BF16),
            pltpu.VMEM((items, slots, hid // 2), BF16),
            pltpu.VMEM((items, slots, hid // 2), BF16),
            pltpu.VMEM((items, slots, hid // 4), BF16),
            pltpu.VMEM((planes, slots, hid // 4), F32),
            pltpu.VMEM((items, slots, hid), BF16),
            pltpu.VMEM((2, width, hid), BF16),
            pltpu.VMEM((planes, slots, width), BF16),
            pltpu.VMEM((planes, slots, width), BF16),
            pltpu.VMEM((planes, 8, lanes), F32),
            pltpu.VMEM((planes, 8, lanes), F32),
            pltpu.VMEM((SLICES, tok_dev, width), BF16),
            pltpu.VMEM((SLICES, 8, tok_dev), F32),
            pltpu.VMEM((SLICES, 8, tok_dev), F32),
            dma((4,)),
            *pairs,
        ],
        compiler_params=pltpu.CompilerParams(
            collective_id=0, has_side_effects=True, vmem_limit_bytes=56 * 1024 * 1024
        ),
        cost_estimate=pl.CostEstimate(
            flops=12 * planes * slots * width * hid, bytes_accessed=8 * 1024 * 1024, transcendentals=0
        ),
    )(tokens, cotangent, gates, routes.reshape(1, tok_dev), w_up, w_down_t)
    grads = jnp.sum(weight_sums.astype(F32), axis=1)
    grad_gates = gate_sums[0].reshape(tok_dev, top_count) / gates
    return grad_tokens, grad_gates, grads[0], grads[1]


def solution(mesh):
    split = P(("rep", "exp"), None)
    weight_split = P(("exp", "rep"), None)
    return jax.shard_map(
        shards,
        mesh=mesh,
        in_specs=(split, split, split, split, weight_split, weight_split),
        out_specs=(split, split, weight_split, weight_split),
        check_vma=False,
    )
```

time: 213 us -> 134 us (0.63)
  the two profiles are of different devices: /device:TPU:0 before, /device:TPU:8 now
where the time goes in v2:
time: 134 us
  Pallas kernels  124 us (93%)
  other arithmetic  4.64 us (3%)
  local copies, waits for them, and re-layouts  4.61 us (3%)
    pallas_call x1, Pallas kernels, shards(): pl.pallas_call(functools.partial(kernel, n_rep, planes, capacity, slots),...  124 us
    reduce_sum x1, other arithmetic, shards(): grads = jnp.sum(weight_sums.astype(F32), axis=1)  3.44 us

profile of v2, /device:TPU:8, one launch (start us, length us, event | category | flops | bytes accessed | tf_op | source)
XLA Modules:
  0.0 134.2 jit_solution(674145228752493977)
XLA Ops:
  0.6 1.4 %copy.10.gates = f32[128,1]{1,0:T(8,128)} copy(f32[128,1]{0,1:T(1,128)} %param.8) | data formatting | bytes 1024 | tf_op args[2]
  2.0 0.0 copy-start.1
  2.0 124.3 %shard_map.93 = (bf16[128,3584]{1,0:T(8,128)(2,1)}, f32[8,128]{1,0:T(8,128)}, bf16[2,2,448,1024]{3,2,1,0:T(8,128)(2,1)}) custom-call(bf16[128,3584]{1,0:T(8,128)(2,1)} %tokens.1, bf16[128,3584]{1,0:T(8,128)(2,1)} %cot.1, f32[128,1]{1,0:T(8,128)} %copy.10.gates, s32[1,128]{1,0:T(1,128)} %bitcast.7, bf16[448,1024]{1,0:T(8,128)(2,1)} %w_up.1, ...), custom_call_target="tpu_custom_call" | custom-call | flops 6341787648 | bytes 8388608 | tf_op jit(solution)/shard_map/pallas_call | solution.py:410
  126.4 0.0 copy-done.1
  126.4 1.2 bitcast_divide_fusion
  127.6 3.4 %convert_reduce_fusion = f32[2,448,1024]{2,1,0:T(8,128)S(1)} fusion(bf16[2,2,448,1024]{3,2,1,0:T(8,128)(2,1)} %get-tuple-element.9), kind=kLoop, calls=%fused_computation | loop fusion | flops 2752512 | bytes 7340032 | tf_op jit(solution)/shard_map/reduce_sum | solution.py:450
  131.0 0.0 copy-start
  131.0 2.3 %slice_bitcast_fusion = (f32[448,1024]{1,0:T(8,128)}, f32[448,1024]{1,0:T(8,128)}) fusion(f32[2,448,1024]{2,1,0:T(8,128)S(1)} %convert_reduce_fusion), kind=kLoop, calls=%fused_computation.1 | loop fusion | bytes 7340032 | tf_op jit(solution)/shard_map/squeeze | solution.py:452
  133.3 0.0 copy-done
  133.3 0.9 copy.12
Async XLA Ops:
  2.0 124.4 %copy-start.1 = (f32[128,1]{0,1:T(1,128)S(1)}, f32[128,1]{0,1:T(1,128)}, u32[]{:S(2)}) copy-start(f32[128,1]{0,1:T(1,128)} %param.8) | copy-start | bytes 1540
  131.0 2.3 %copy-start = (bf16[128,3584]{1,0:T(8,128)(2,1)S(1)}, bf16[128,3584]{1,0:T(8,128)(2,1)}, u32[]{:S(2)}) copy-start(bf16[128,3584]{1,0:T(8,128)(2,1)} %get-tuple-element.16) | copy-start | bytes 2752516

commit v3 on v2

--- a/solution.py
+++ b/solution.py
@@ -25,8 +25,8 @@
 def kernel(
     n_rep, planes, capacity, slots,
     tokens, cot, gates, routes, w_up, w_down,
-    grad_tokens, gate_sums, weight_sums,
-    out_grad, raw, place, weights, packed, rows, part, first, first_in, second_in,
+    grad_tokens, gate_sums, up_sums, down_sums,
+    cot_block, out_grad, raw, place, weights, packed, rows, part, first, first_in, second_in,
     act, hidden, terms, dx, dx_in, gate_row, gate_in, back, gate_back, gate_mates,
     local_sem, raw_send, raw_recv, place_send, place_recv, weight_send, weight_recv,
     plane_send, plane_recv, a_send, a_recv, b_send, b_recv, c_send, c_recv, d_send, d_recv,
@@ -36,10 +36,12 @@
     rep, me = lax.axis_index("rep"), lax.axis_index("exp")
     plane, q = me // SLICES, me % SLICES
     low, high = q % 2, q // 2
-    tok_dev, width = tokens.shape[0], raw.shape[3]
+    tok_dev, width = raw.shape[2], raw.shape[3]
     own_rows, hid = w_up.shape
     half, quarter = hid // 2, hid // 4
     items = 2 * planes
+    hops = planes - 1
+    last_slot = planes + 4 * hops
 
     def mate(distance):
         return (rep, plane * SLICES + (q + distance) % SLICES)
@@ -117,7 +119,7 @@
 
     def term_copy(a, d):
         return copy(
-            terms.at[a, weight_rows((rep + d) % n_rep)], weight_sums.at[a, d],
+            terms.at[a, weight_rows((rep + d) % n_rep)], (up_sums, down_sums)[a].at[d],
             term_send.at[a, d], term_recv.at[a, d], replica(d),
         )
 
@@ -130,6 +132,13 @@
     def mate_copy(j):
         return copy(gate_back.at[j], gate_mates.at[j], mate_send.at[j], mate_recv.at[j], mate(j))
 
+    def term_local(a):
+        return pltpu.make_async_copy(
+            terms.at[a, weight_rows(rep)], (up_sums, down_sums)[a].at[0], local_sem.at[a]
+        )
+
+    cot_local = pltpu.make_async_copy(cot, cot_block, local_sem.at[4])
+    cot_local.start()
     barrier = pltpu.get_barrier_semaphore()
     peers = [mate(j) for j in range(1, SLICES)] + [replica(d) for d in range(1, n_rep)]
     for device in peers:
@@ -166,14 +175,14 @@
     for j in range(1, SLICES):
         place_copy(j).start()
 
-    gate = gates[...]
+    square = lax.broadcasted_iota(jnp.int32, (tok_dev, tok_dev), 0) == lax.broadcasted_iota(
+        jnp.int32, (tok_dev, tok_dev), 1
+    )
+    gate = jnp.sum(jnp.where(square, gates[...], 0.0), axis=1, keepdims=True)
+    cot_local.wait()
     for m in range(SLICES):
         block = slice(m * width, (m + 1) * width)
-        out_grad[:, block] = (gate * cot[:, block].astype(F32)).astype(BF16)
-    for j in range(1, SLICES):
-        raw_copy(1, j).start()
-    for d in range(1, n_rep):
-        weight_copy(1, d).start()
+        out_grad[:, block] = (gate * cot_block[:, block].astype(F32)).astype(BF16)
     local_grad = pltpu.make_async_copy(
         out_grad.at[:, feature_block(q)], raw.at[1, q], local_sem.at[3]
     )
@@ -201,11 +210,17 @@
                 raw.at[a, sender], raw.at[a, sender], raw_send.at[a, j], raw_recv.at[a, j], mate(j)
             ).wait_recv()
         (local[0], local_grad)[a].wait()
+        if a == 0:
+            for j in range(1, SLICES):
+                raw_copy(1, j).start()
 
         @pl.loop(1, planes)
         def _(k):
             pack(a, k, packed)
-            plane_copy(a, k).start()
+            if a == 0:
+                @pl.when(k < 3)
+                def _():
+                    plane_copy(0, k).start()
 
         pack(a, 0, rows)
     local[1].wait()
@@ -223,36 +238,21 @@
 
         for d in range(1, n_rep):
             term_copy(a, d).start()
-        weight_sums[a, 0] = terms[a, weight_rows(rep), :]
-
-    @pl.loop(0, items + 4)
+        term_local(a).start()
+
+    @pl.loop(0, last_slot + 5)
     def _(s):
-        @pl.when(s < items)
+        def stage(lag):
+            slot = s - lag
+            extra = slot - planes
+            item = jnp.where(extra > 0, planes + extra // 4, slot)
+            return item, (slot >= 0) & (slot <= last_slot) & ((extra <= 0) | (extra % 4 == 0))
+
+        e_item, e_here = stage(4)
+
+        @pl.when(e_here)
         def _():
-            a, k = s // planes, s % planes
-
-            @pl.when(k == 0)
-            def _():
-                for d in range(1, n_rep):
-                    landed = weights.at[a, weight_rows((rep + n_rep - d) % n_rep)]
-                    copy(
-                        landed, landed, weight_send.at[a, d], weight_recv.at[a, d], replica(d)
-                    ).wait_recv()
-
-            @pl.when(k > 0)
-            def _():
-                plane_copy(a, k).wait_recv()
-
-            left = rows[a, k]
-            for start, size in tiles(hid):
-                part[s, :, start : start + size] = dot(
-                    left, weights[a, :, start : start + size], (1, 0)
-                ).astype(BF16)
-            a_copy(s).start()
-
-        @pl.when(s >= 4)
-        def _():
-            t = s - 4
+            t = e_item
             landed = hidden.at[t, :, pl.ds(pl.multiple_of((1 - low) * half, 128), half)]
             copy(landed, landed, d_send.at[t], d_recv.at[t], near).wait_recv()
 
@@ -270,18 +270,22 @@
                     gate_copy(k).start()
                     dx_copy(k).start()
 
-        @pl.when((s >= 3) & (s < items + 3))
+        d_item, d_here = stage(3)
+
+        @pl.when(d_here)
         def _():
-            t = s - 3
+            t = d_item
             landed = hidden.at[
                 t, :, pl.ds(pl.multiple_of(low * half + (1 - high) * quarter, 128), quarter)
             ]
             copy(landed, landed, c_send.at[t], c_recv.at[t], far).wait_recv()
             d_copy(t).start()
 
-        @pl.when((s >= 2) & (s < items + 2))
+        c_item, c_here = stage(2)
+
+        @pl.when(c_here)
         def _():
-            t = s - 2
+            t = c_item
             b_copy(t).wait_recv()
             mine = pl.ds(pl.multiple_of(high * quarter, 128), quarter)
             total = first[t, :, mine].astype(F32) + second_in[t].astype(F32)
@@ -306,14 +310,51 @@
 
             c_copy(t).start()
 
-        @pl.when((s >= 1) & (s < items + 1))
+        b_item, b_here = stage(1)
+
+        @pl.when(b_here)
         def _():
-            t = s - 1
+            t = b_item
             a_copy(t).wait_recv()
             first[t] = (part[t, :, own_half].astype(F32) + first_in[t].astype(F32)).astype(BF16)
             b_copy(t).start()
 
-        @pl.when(s == items)
+        i, here = stage(0)
+
+        @pl.when(here)
+        def _():
+            a, k = i // planes, i % planes
+
+            @pl.when(k == 0)
+            def _():
+                for d in range(1, n_rep):
+                    landed = weights.at[a, weight_rows((rep + n_rep - d) % n_rep)]
+                    copy(
+                        landed, landed, weight_send.at[a, d], weight_recv.at[a, d], replica(d)
+                    ).wait_recv()
+
+                @pl.when(a == 0)
+                def _():
+                    for d in range(1, n_rep):
+                        weight_copy(1, d).start()
+
+            @pl.when(k > 0)
+            def _():
+                plane_copy(a, k).wait_recv()
+                later = a * hops + k + 1
+
+                @pl.when(later < 2 * hops)
+                def _():
+                    plane_copy(later // hops, later % hops + 1).start()
+
+            left = rows[a, k]
+            for start, size in tiles(hid):
+                part[i, :, start : start + size] = dot(
+                    left, weights[a, :, start : start + size], (1, 0)
+                ).astype(BF16)
+            a_copy(i).start()
+
+        @pl.when(s == last_slot + 1)
         def _():
             weight_term(1)
 
@@ -346,19 +387,20 @@
             back_copy(j).start()
             mate_copy(j).start()
     last = pltpu.make_async_copy(
-        back.at[0], grad_tokens.at[:, feature_block(q)], local_sem.at[0]
+        back.at[0], grad_tokens.at[:, feature_block(q)], local_sem.at[2]
     )
     last.start()
     total = gate_back[0]
     for j in range(1, SLICES):
         mate_copy(j).wait_recv()
         total += gate_mates[j]
-    gate_sums[...] = total
+    gate_sums[...] = total[0:1] / gates[...]
     last.wait()
     for j in range(1, SLICES):
         landed = grad_tokens.at[:, feature_block((q + SLICES - j) % SLICES)]
         copy(landed, landed, back_send.at[j], back_recv.at[j], mate(j)).wait_recv()
     for a in range(2):
+        term_local(a).wait()
         for d in range(1, n_rep):
             term_copy(a, d).wait_recv()
             term_copy(a, d).wait_send()
@@ -401,22 +443,25 @@
     items = 2 * planes
     dma = pltpu.SemaphoreType.DMA
     vmem = pl.BlockSpec(memory_space=pltpu.VMEM)
+    hbm = pl.BlockSpec(memory_space=pl.ANY)
     pairs = []
     for shape in (
         (2, SLICES), (SLICES,), (2, n_rep), (2, planes), (items,), (items,), (items,), (items,),
         (planes,), (planes,), (2, n_rep), (SLICES,), (SLICES,),
     ):
         pairs += [dma(shape), dma(shape)]
-    grad_tokens, gate_sums, weight_sums = pl.pallas_call(
+    grad_tokens, gate_sums, up_sums, down_sums = pl.pallas_call(
         functools.partial(kernel, n_rep, planes, capacity, slots),
         out_shape=(
             jax.ShapeDtypeStruct((tok_dev, model_width), BF16),
-            jax.ShapeDtypeStruct((8, tok_dev), F32),
-            jax.ShapeDtypeStruct((2, n_rep, own_rows, hid), BF16),
+            jax.ShapeDtypeStruct((1, tok_dev), F32),
+            jax.ShapeDtypeStruct((n_rep, own_rows, hid), BF16),
+            jax.ShapeDtypeStruct((n_rep, own_rows, hid), BF16),
         ),
-        in_specs=[vmem] * 6,
-        out_specs=(vmem, vmem, vmem),
+        in_specs=[hbm, hbm, vmem, vmem, hbm, hbm],
+        out_specs=(hbm, vmem, hbm, hbm),
         scratch_shapes=[
+            pltpu.VMEM((tok_dev, model_width), BF16),
             pltpu.VMEM((tok_dev, model_width), BF16),
             pltpu.VMEM((2, SLICES, tok_dev, width), BF16),
             pltpu.VMEM((SLICES, 8, tok_dev), F32),
@@ -437,7 +482,7 @@
             pltpu.VMEM((SLICES, tok_dev, width), BF16),
             pltpu.VMEM((SLICES, 8, tok_dev), F32),
             pltpu.VMEM((SLICES, 8, tok_dev), F32),
-            dma((4,)),
+            dma((5,)),
             *pairs,
         ],
         compiler_params=pltpu.CompilerParams(
@@ -446,10 +491,10 @@
         cost_estimate=pl.CostEstimate(
             flops=12 * planes * slots * width * hid, bytes_accessed=8 * 1024 * 1024, transcendentals=0
         ),
-    )(tokens, cotangent, gates, routes.reshape(1, tok_dev), w_up, w_down_t)
-    grads = jnp.sum(weight_sums.astype(F32), axis=1)
-    grad_gates = gate_sums[0].reshape(tok_dev, top_count) / gates
-    return grad_tokens, grad_gates, grads[0], grads[1]
+    )(tokens, cotangent, gates.reshape(1, tok_dev), routes.reshape(1, tok_dev), w_up, w_down_t)
+    grad_up = jnp.sum(up_sums.astype(F32), axis=0)
+    grad_down_t = jnp.sum(down_sums.astype(F32), axis=0)
+    return grad_tokens, gate_sums.reshape(tok_dev, top_count), grad_up, grad_down_t
 
 
 def solution(mesh):

time: 134 us -> 137 us (1.022)
  the two profiles are of different devices: /device:TPU:8 before, /device:TPU:0 now
where the time goes in v3:
time: 137 us; the launch traced here: 136 us
  Pallas kernels  129 us (94%)
  other arithmetic  5.2 us (4%)
  local copies, waits for them, and re-layouts  1.44 us (1%)
    pallas_call x1, Pallas kernels, shards(): pl.pallas_call(functools.partial(kernel, n_rep, planes, capacity, slots),...  129 us
    reduce_sum x1, other arithmetic, shards(): grad_down_t = jnp.sum(down_sums.astype(F32), axis=0)  5.2 us

profile of v3, /device:TPU:0, one launch (start us, length us, event | category | flops | bytes accessed | tf_op | source)
XLA Modules:
  0.0 135.9 jit_solution(4791465587687665134)
XLA Ops:
  0.6 128.6 %shard_map.93 = (bf16[128,3584]{1,0:T(8,128)(2,1)}, f32[1,128]{1,0:T(1,128)}, bf16[2,448,1024]{2,1,0:T(8,128)(2,1)}, bf16[2,448,1024]{2,1,0:T(8,128)(2,1)}) custom-call(bf16[128,3584]{1,0:T(8,128)(2,1)} %tokens.1, bf16[128,3584]{1,0:T(8,128)(2,1)} %cot.1, f32[1,128]{1,0:T(1,128)} %bitcast.3, s32[1,128]{1,0:T(1,128)} %bitcast.4, bf16[448,1024]{1,0:T(8,128)(2,1)} %w_up.1, ...), custom_call_target="tpu_custom_call" | custom-call | flops 6341787648 | bytes 8388608 | tf_op jit(solution)/shard_map/pallas_call | solution.py:453
  129.3 0.0 copy-start
  129.3 5.2 %convert_reduce_fusion = (f32[448,1024]{1,0:T(8,128)}, f32[448,1024]{1,0:T(8,128)}) fusion(bf16[2,448,1024]{2,1,0:T(8,128)(2,1)} %get-tuple-element.11, bf16[2,448,1024]{2,1,0:T(8,128)(2,1)} %get-tuple-element.10), kind=kLoop, calls=%fused_computation | loop fusion | flops 2752512 | bytes 7340032 | tf_op jit(solution)/shard_map/reduce_sum | solution.py:496
  134.5 0.0 copy-start.1
  134.5 0.0 copy-done
  134.5 0.9 copy.12
  135.4 0.0 copy-done.1
  135.4 0.5 copy.13
Async XLA Ops:
  129.3 5.2 %copy-start = (bf16[128,3584]{1,0:T(8,128)(2,1)S(1)}, bf16[128,3584]{1,0:T(8,128)(2,1)}, u32[]{:S(2)}) copy-start(bf16[128,3584]{1,0:T(8,128)(2,1)} %get-tuple-element.18) | copy-start | bytes 2752516
  134.5 0.9 copy-start.1

commit v4 on v3

--- a/solution.py
+++ b/solution.py
@@ -41,7 +41,7 @@
     half, quarter = hid // 2, hid // 4
     items = 2 * planes
     hops = planes - 1
-    last_slot = planes + 4 * hops
+    last_slot = planes + 2 * hops
 
     def mate(distance):
         return (rep, plane * SLICES + (q + distance) % SLICES)
@@ -217,25 +217,21 @@
         @pl.loop(1, planes)
         def _(k):
             pack(a, k, packed)
-            if a == 0:
-                @pl.when(k < 3)
-                def _():
-                    plane_copy(0, k).start()
+            plane_copy(a, k).start()
 
         pack(a, 0, rows)
     local[1].wait()
     local[2].wait()
 
+    def split(value):
+        upper = value.astype(BF16)
+        return upper, (value - upper.astype(F32)).astype(BF16)
+
     def weight_term(a):
-        @pl.loop(0, width // 128)
-        def _(i):
-            features = pl.ds(pl.multiple_of(i * 128, 128), 128)
-            left = rows[a, :, :, features].reshape(planes * slots, 128)
-            for start, size in tiles(hid, 512):
-                right = hidden[(1 - a) * planes : (2 - a) * planes, :, start : start + size]
-                right = right.reshape(planes * slots, size)
-                terms[a, features, start : start + size] = dot(left, right, (0, 0)).astype(BF16)
-
+        right = hidden[(1 - a) * planes : (2 - a) * planes].reshape(planes * slots, hid)
+        for start, size in tiles(width, 512):
+            left = rows[a, :, :, start : start + size].reshape(planes * slots, size)
+            terms[a, start : start + size, :] = dot(left, right, (0, 0)).astype(BF16)
         for d in range(1, n_rep):
             term_copy(a, d).start()
         term_local(a).start()
@@ -245,8 +241,8 @@
         def stage(lag):
             slot = s - lag
             extra = slot - planes
-            item = jnp.where(extra > 0, planes + extra // 4, slot)
-            return item, (slot >= 0) & (slot <= last_slot) & ((extra <= 0) | (extra % 4 == 0))
+            item = jnp.where(extra > 0, planes + extra // 2, slot)
+            return item, (slot >= 0) & (slot <= last_slot) & ((extra <= 0) | (extra % 2 == 0))
 
         e_item, e_here = stage(4)
 
@@ -303,10 +299,10 @@
                 hidden[t, :, own_quarter] = (
                     total * gating * (1.0 + value * (1.0 - gating))
                 ).astype(BF16)
-                gate_row[k, :, 0:slots] = dot(
-                    jnp.ones((8, quarter), F32), total * (value * gating), (1, 1),
-                    lax.Precision.HIGHEST,
-                )
+                upper, lower = split(total * (value * gating))
+                ones = jnp.ones((16, quarter), BF16)
+                sums = dot(ones, upper, (1, 1)) + dot(ones, lower, (1, 1))
+                gate_row[k, :, 0:slots] = sums[0:8]
 
             c_copy(t).start()
 
@@ -341,11 +337,6 @@
             @pl.when(k > 0)
             def _():
                 plane_copy(a, k).wait_recv()
-                later = a * hops + k + 1
-
-                @pl.when(later < 2 * hops)
-                def _():
-                    plane_copy(later // hops, later % hops + 1).start()
 
             left = rows[a, k]
             for start, size in tiles(hid):
@@ -378,10 +369,9 @@
             back[j, :, start : start + size] = dot(matrix, landed, (0, 0)).astype(BF16)
         sums = jnp.zeros((8, tok_dev), F32)
         for k in range(planes):
-            source = gate_row if k == 0 else gate_in
-            sums += dot(
-                source[k, :, 0:slots], blocks[k].astype(F32), (1, 0), lax.Precision.HIGHEST
-            )
+            upper, lower = split((gate_row if k == 0 else gate_in)[k, :, 0:slots])
+            both = dot(jnp.concatenate([upper, lower], axis=0), blocks[k], (1, 0))
+            sums += both[0:8] + both[8:16]
         gate_back[j] = sums
         if j > 0:
             back_copy(j).start()
@@ -492,8 +482,8 @@
             flops=12 * planes * slots * width * hid, bytes_accessed=8 * 1024 * 1024, transcendentals=0
         ),
     )(tokens, cotangent, gates.reshape(1, tok_dev), routes.reshape(1, tok_dev), w_up, w_down_t)
-    grad_up = jnp.sum(up_sums.astype(F32), axis=0)
-    grad_down_t = jnp.sum(down_sums.astype(F32), axis=0)
+    grad_up = sum(up_sums[d].astype(F32) for d in range(n_rep))
+    grad_down_t = sum(down_sums[d].astype(F32) for d in range(n_rep))
     return grad_tokens, gate_sums.reshape(tok_dev, top_count), grad_up, grad_down_t
 
 

time: 137 us -> 130 us (0.949)
  the two profiles are of different devices: /device:TPU:0 before, /device:TPU:8 now
where the time goes in v4:
time: 130 us
  Pallas kernels  123 us (95%)
  other arithmetic  4.69 us (4%)
  local copies, waits for them, and re-layouts  1.44 us (1%)
    pallas_call x1, Pallas kernels, shards(): pl.pallas_call(functools.partial(kernel, n_rep, planes, capacity, slots),...  123 us
    add x1, other arithmetic, shards(): grad_down_t = sum((down_sums[d].astype(F32) for d in range(n_rep)))  4.69 us

profile of v4, /device:TPU:8, one launch (start us, length us, event | category | flops | bytes accessed | tf_op | source)
XLA Modules:
  0.0 130.0 jit_solution(7869507646128557710)
XLA Ops:
  0.6 123.2 %shard_map.93 = (bf16[128,3584]{1,0:T(8,128)(2,1)}, f32[1,128]{1,0:T(1,128)}, bf16[2,448,1024]{2,1,0:T(8,128)(2,1)}, bf16[2,448,1024]{2,1,0:T(8,128)(2,1)}) custom-call(bf16[128,3584]{1,0:T(8,128)(2,1)} %tokens.1, bf16[128,3584]{1,0:T(8,128)(2,1)} %cot.1, f32[1,128]{1,0:T(1,128)} %bitcast.7, s32[1,128]{1,0:T(1,128)} %bitcast.8, bf16[448,1024]{1,0:T(8,128)(2,1)} %w_up.1, ...), custom_call_target="tpu_custom_call" | custom-call | flops 6341787648 | bytes 8388608 | tf_op jit(solution)/shard_map/pallas_call | solution.py:443
  123.8 0.0 copy-start
  123.8 4.7 %add_bitcast_fusion = (f32[448,1024]{1,0:T(8,128)}, f32[448,1024]{1,0:T(8,128)}) fusion(bf16[2,448,1024]{2,1,0:T(8,128)(2,1)} %get-tuple-element.11, bf16[2,448,1024]{2,1,0:T(8,128)(2,1)} %get-tuple-element.10), kind=kLoop, calls=%fused_computation | loop fusion | flops 2752512 | bytes 7340032 | tf_op jit(solution)/shard_map/add | solution.py:486
  128.5 0.0 copy-start.1
  128.5 0.0 copy-done
  128.5 0.9 copy.12
  129.4 0.0 copy-done.1
  129.5 0.5 copy.13
Async XLA Ops:
  123.8 4.7 %copy-start = (bf16[128,3584]{1,0:T(8,128)(2,1)S(1)}, bf16[128,3584]{1,0:T(8,128)(2,1)}, u32[]{:S(2)}) copy-start(bf16[128,3584]{1,0:T(8,128)(2,1)} %get-tuple-element.18) | copy-start | bytes 2752516
  128.5 0.9 copy-start.1

commit v5 on v4

--- a/solution.py
+++ b/solution.py
@@ -23,15 +23,16 @@
 
 
 def kernel(
-    n_rep, planes, capacity, slots,
+    n_rep, planes, capacity, slots, pair, cover,
     tokens, cot, gates, routes, w_up, w_down,
     grad_tokens, gate_sums, up_sums, down_sums,
     cot_block, out_grad, raw, place, weights, packed, rows, part, first, first_in, second_in,
     act, hidden, terms, dx, dx_in, gate_row, gate_in, back, gate_back, gate_mates,
+    rows_peer, hidden_peer,
     local_sem, raw_send, raw_recv, place_send, place_recv, weight_send, weight_recv,
     plane_send, plane_recv, a_send, a_recv, b_send, b_recv, c_send, c_recv, d_send, d_recv,
     dx_send, dx_recv, gate_send, gate_recv, term_send, term_recv, back_send, back_recv,
-    mate_send, mate_recv,
+    mate_send, mate_recv, y_send, y_recv, h_send, h_recv, f_send, f_recv, g_send, g_recv,
 ):
     rep, me = lax.axis_index("rep"), lax.axis_index("exp")
     plane, q = me // SLICES, me % SLICES
@@ -41,6 +42,7 @@
     half, quarter = hid // 2, hid // 4
     items = 2 * planes
     hops = planes - 1
+    parts = tiles(width, 512)
     last_slot = planes + 2 * hops
 
     def mate(distance):
@@ -70,11 +72,19 @@
     def weight_rows(index):
         return pl.ds(pl.multiple_of(index * own_rows, 16), own_rows)
 
-    def raw_copy(a, j):
+    def feature_part(index, p):
+        start, size = parts[p]
+        return pl.ds(pl.multiple_of(index * width + start, 128), size)
+
+    def inner(p):
+        start, size = parts[p]
+        return slice(start, start + size)
+
+    def raw_copy(a, j, p):
         source = (tokens, out_grad)[a]
         return copy(
-            source.at[:, feature_block((q + j) % SLICES)], raw.at[a, q],
-            raw_send.at[a, j], raw_recv.at[a, j], mate(j),
+            source.at[:, feature_part((q + j) % SLICES, p)], raw.at[a, q, :, inner(p)],
+            raw_send.at[a, p, j], raw_recv.at[a, p, j], mate(j),
         )
 
     def place_copy(j):
@@ -87,9 +97,10 @@
             weight_send.at[a, d], weight_recv.at[a, d], replica(d),
         )
 
-    def plane_copy(a, k):
-        return copy(
-            packed.at[a, k], rows.at[a, k], plane_send.at[a, k], plane_recv.at[a, k], ahead(k)
+    def plane_copy(a, k, p):
+        return copy(
+            packed.at[a, k, :, inner(p)], rows.at[a, k, :, inner(p)],
+            plane_send.at[a, p, k], plane_recv.at[a, p, k], ahead(k),
         )
 
     def a_copy(s):
@@ -111,8 +122,34 @@
         block = hidden.at[s, :, own_half]
         return copy(block, block, d_send.at[s], d_recv.at[s], near)
 
-    def dx_copy(k):
-        return copy(dx.at[k], dx_in.at[k], dx_send.at[k], dx_recv.at[k], behind(k))
+    def dx_copy(k, p):
+        return copy(
+            dx.at[k, :, inner(p)], dx_in.at[k, :, inner(p)],
+            dx_send.at[p, k], dx_recv.at[p, k], behind(k),
+        )
+
+    def cover_start(replica_index):
+        return jnp.minimum(replica_index * own_rows // 128 * 128, width - cover)
+
+    def y_copy(a, k):
+        block = pl.ds(pl.multiple_of(cover_start((rep + 1) % n_rep), 128), cover)
+        return copy(
+            rows.at[a, k, :, block], rows_peer.at[a, k], y_send.at[a, k], y_recv.at[a, k], replica(1)
+        )
+
+    def h_copy(t):
+        return copy(
+            hidden.at[t, :, own_quarter], hidden_peer.at[t, :, own_quarter],
+            h_send.at[t], h_recv.at[t], replica(1),
+        )
+
+    def f_copy(t):
+        block = hidden_peer.at[t, :, own_quarter]
+        return copy(block, block, f_send.at[t], f_recv.at[t], far)
+
+    def g_copy(t):
+        block = hidden_peer.at[t, :, own_half]
+        return copy(block, block, g_send.at[t], g_recv.at[t], near)
 
     def gate_copy(k):
         return copy(gate_row.at[k], gate_in.at[k], gate_send.at[k], gate_recv.at[k], behind(k))
@@ -123,18 +160,21 @@
             term_send.at[a, d], term_recv.at[a, d], replica(d),
         )
 
-    def back_copy(j):
-        return copy(
-            back.at[j], grad_tokens.at[:, feature_block(q)],
-            back_send.at[j], back_recv.at[j], mate(j),
+    def back_copy(j, p):
+        return copy(
+            back.at[j, :, inner(p)], grad_tokens.at[:, feature_part(q, p)],
+            back_send.at[p, j], back_recv.at[p, j], mate(j),
         )
 
     def mate_copy(j):
         return copy(gate_back.at[j], gate_mates.at[j], mate_send.at[j], mate_recv.at[j], mate(j))
 
     def term_local(a):
+        kept = weight_rows(rep)
+        if pair:
+            kept = pl.ds(pl.multiple_of(rep * own_rows - cover_start(rep), 16), own_rows)
         return pltpu.make_async_copy(
-            terms.at[a, weight_rows(rep)], (up_sums, down_sums)[a].at[0], local_sem.at[a]
+            terms.at[a, kept], (up_sums, down_sums)[a].at[0], local_sem.at[a]
         )
 
     cot_local = pltpu.make_async_copy(cot, cot_block, local_sem.at[4])
@@ -151,7 +191,7 @@
     pl.semaphore_wait(barrier, len(peers) + planes - 1)
 
     for j in range(1, SLICES):
-        raw_copy(0, j).start()
+        raw_copy(0, j, 0).start()
     for d in range(1, n_rep):
         weight_copy(0, d).start()
     local = [
@@ -174,6 +214,9 @@
     place[q] = jnp.broadcast_to(position, (8, tok_dev))
     for j in range(1, SLICES):
         place_copy(j).start()
+    for p in range(1, len(parts)):
+        for j in range(1, SLICES):
+            raw_copy(0, j, p).start()
 
     square = lax.broadcasted_iota(jnp.int32, (tok_dev, tok_dev), 0) == lax.broadcasted_iota(
         jnp.int32, (tok_dev, tok_dev), 1
@@ -197,31 +240,43 @@
         number = lax.broadcasted_iota(jnp.int32, (slots, positions.shape[1]), 0) + expert * slots
         return jnp.where(number.astype(F32) == positions, 1.0, 0.0).astype(kind)
 
-    def pack(a, k, target):
+    def pack(a, k, p, target):
         matrix = chosen((plane + k) % planes, places, BF16)
-        for start, size in tiles(width):
-            source = raw[a, :, :, start : start + size].reshape(SLICES * tok_dev, size)
-            target[a, k, :, start : start + size] = dot(matrix, source, (1, 0)).astype(BF16)
+        begin, length = parts[p]
+        for start, size in tiles(length):
+            block = slice(begin + start, begin + start + size)
+            source = raw[a, :, :, block].reshape(SLICES * tok_dev, size)
+            target[a, k, :, block] = dot(matrix, source, (1, 0)).astype(BF16)
 
     for a in range(2):
-        for j in range(1, SLICES):
-            sender = (q + SLICES - j) % SLICES
-            copy(
-                raw.at[a, sender], raw.at[a, sender], raw_send.at[a, j], raw_recv.at[a, j], mate(j)
-            ).wait_recv()
         (local[0], local_grad)[a].wait()
-        if a == 0:
+        for p in range(len(parts)):
             for j in range(1, SLICES):
-                raw_copy(1, j).start()
-
-        @pl.loop(1, planes)
-        def _(k):
-            pack(a, k, packed)
-            plane_copy(a, k).start()
-
-        pack(a, 0, rows)
+                landed = raw.at[a, (q + SLICES - j) % SLICES, :, inner(p)]
+                copy(
+                    landed, landed, raw_send.at[a, p, j], raw_recv.at[a, p, j], mate(j)
+                ).wait_recv()
+            if a == 0:
+                for j in range(1, SLICES):
+                    raw_copy(1, j, p).start()
+
+            @pl.loop(1, planes)
+            def _(k):
+                pack(a, k, p, packed)
+                plane_copy(a, k, p).start()
+
+            pack(a, 0, p, rows)
+        if pair:
+            y_copy(a, 0).start()
     local[1].wait()
     local[2].wait()
+
+    def dx_product(k, p):
+        left = hidden[planes + k]
+        begin, length = parts[p]
+        for start, size in tiles(length):
+            block = slice(begin + start, begin + start + size)
+            dx[k, :, block] = dot(left, weights[0, block, :], (1, 1)).astype(BF16)
 
     def split(value):
         upper = value.astype(BF16)
@@ -236,7 +291,7 @@
             term_copy(a, d).start()
         term_local(a).start()
 
-    @pl.loop(0, last_slot + 5)
+    @pl.loop(0, last_slot + (9 if pair else 6))
     def _(s):
         def stage(lag):
             slot = s - lag
@@ -255,16 +310,12 @@
             @pl.when(t >= planes)
             def _():
                 k = t - planes
-                left = hidden[t]
-                for start, size in tiles(width):
-                    dx[k, :, start : start + size] = dot(
-                        left, weights[0, start : start + size, :], (1, 1)
-                    ).astype(BF16)
+                dx_product(k, 0)
 
                 @pl.when(k > 0)
                 def _():
                     gate_copy(k).start()
-                    dx_copy(k).start()
+                    dx_copy(k, 0).start()
 
         d_item, d_here = stage(3)
 
@@ -305,6 +356,8 @@
                 gate_row[k, :, 0:slots] = sums[0:8]
 
             c_copy(t).start()
+            if pair:
+                h_copy(t).start()
 
         b_item, b_here = stage(1)
 
@@ -336,7 +389,10 @@
 
             @pl.when(k > 0)
             def _():
-                plane_copy(a, k).wait_recv()
+                for p in range(len(parts)):
+                    plane_copy(a, k, p).wait_recv()
+                if pair:
+                    y_copy(a, k).start()
 
             left = rows[a, k]
             for start, size in tiles(hid):
@@ -345,37 +401,97 @@
                 ).astype(BF16)
             a_copy(i).start()
 
-        @pl.when(s == last_slot + 1)
+        @pl.when(s == last_slot + 5)
         def _():
-            weight_term(1)
-
-    weight_term(0)
+            for p in range(1, len(parts)):
+                dx_product(0, p)
+
+                @pl.loop(1, planes)
+                def _(k):
+                    dx_product(k, p)
+                    dx_copy(k, p).start()
+
+        if pair:
+            f_item, f_here = stage(6)
+
+            @pl.when(f_here)
+            def _():
+                h_copy(f_item).wait_recv()
+                f_copy(f_item).start()
+
+            g_item, g_here = stage(8)
+
+            @pl.when(g_here)
+            def _():
+                t = g_item
+                landed = hidden_peer.at[
+                    t, :, pl.ds(pl.multiple_of(low * half + (1 - high) * quarter, 128), quarter)
+                ]
+                copy(landed, landed, f_send.at[t], f_recv.at[t], far).wait_recv()
+                g_copy(t).start()
+        else:
+            @pl.when(s == last_slot + 1)
+            def _():
+                weight_term(1)
+
+    def pair_term(a):
+        @pl.loop((1 - a) * planes, (2 - a) * planes)
+        def _(t):
+            landed = hidden_peer.at[t, :, pl.ds(pl.multiple_of((1 - low) * half, 128), half)]
+            copy(landed, landed, g_send.at[t], g_recv.at[t], near).wait_recv()
+
+        @pl.loop(0, planes)
+        def _(k):
+            landed = rows_peer.at[a, k]
+            copy(landed, landed, y_send.at[a, k], y_recv.at[a, k], replica(1)).wait_recv()
+
+        count = planes * slots
+        mine = pl.ds(pl.multiple_of(cover_start(rep), 128), cover)
+        some = slice((1 - a) * planes, (2 - a) * planes)
+        total = dot(
+            rows[a, :, :, mine].reshape(count, cover), hidden[some].reshape(count, hid), (0, 0)
+        )
+        total += dot(
+            rows_peer[a].reshape(count, cover), hidden_peer[some].reshape(count, hid), (0, 0)
+        )
+        terms[a] = total.astype(BF16)
+        term_local(a).start()
+
+    if pair:
+        pair_term(1)
+        pair_term(0)
+    else:
+        weight_term(0)
 
     @pl.loop(1, planes)
     def _(k):
         gate_copy(k).wait_recv()
-        dx_copy(k).wait_recv()
-
-    for j in (2, 1, 3, 0):
-        positions = place[(q + j) % SLICES][0:1, :]
-        blocks = [chosen((plane + k) % planes, positions, BF16) for k in range(planes)]
-        matrix = jnp.concatenate(blocks, axis=0)
-        for start, size in tiles(width):
+
+    for p in range(len(parts)):
+        @pl.loop(1, planes)
+        def _(k):
+            dx_copy(k, p).wait_recv()
+
+        for j in (2, 1, 3, 0):
+            positions = place[(q + j) % SLICES][0:1, :]
+            blocks = [chosen((plane + k) % planes, positions, BF16) for k in range(planes)]
+            matrix = jnp.concatenate(blocks, axis=0)
             landed = jnp.concatenate(
-                [dx[0, :, start : start + size]]
-                + [dx_in[k, :, start : start + size] for k in range(1, planes)],
-                axis=0,
+                [dx[0, :, inner(p)]] + [dx_in[k, :, inner(p)] for k in range(1, planes)], axis=0
             )
-            back[j, :, start : start + size] = dot(matrix, landed, (0, 0)).astype(BF16)
-        sums = jnp.zeros((8, tok_dev), F32)
-        for k in range(planes):
-            upper, lower = split((gate_row if k == 0 else gate_in)[k, :, 0:slots])
-            both = dot(jnp.concatenate([upper, lower], axis=0), blocks[k], (1, 0))
-            sums += both[0:8] + both[8:16]
-        gate_back[j] = sums
-        if j > 0:
-            back_copy(j).start()
-            mate_copy(j).start()
+            back[j, :, inner(p)] = dot(matrix, landed, (0, 0)).astype(BF16)
+            if j > 0:
+                back_copy(j, p).start()
+            if p > 0:
+                continue
+            sums = jnp.zeros((8, tok_dev), F32)
+            for k in range(planes):
+                upper, lower = split((gate_row if k == 0 else gate_in)[k, :, 0:slots])
+                both = dot(jnp.concatenate([upper, lower], axis=0), blocks[k], (1, 0))
+                sums += both[0:8] + both[8:16]
+            gate_back[j] = sums
+            if j > 0:
+                mate_copy(j).start()
     last = pltpu.make_async_copy(
         back.at[0], grad_tokens.at[:, feature_block(q)], local_sem.at[2]
     )
@@ -386,30 +502,35 @@
         total += gate_mates[j]
     gate_sums[...] = total[0:1] / gates[...]
     last.wait()
-    for j in range(1, SLICES):
-        landed = grad_tokens.at[:, feature_block((q + SLICES - j) % SLICES)]
-        copy(landed, landed, back_send.at[j], back_recv.at[j], mate(j)).wait_recv()
+    for p in range(len(parts)):
+        for j in range(1, SLICES):
+            landed = grad_tokens.at[:, feature_part((q + SLICES - j) % SLICES, p)]
+            copy(landed, landed, back_send.at[p, j], back_recv.at[p, j], mate(j)).wait_recv()
+            back_copy(j, p).wait_send()
     for a in range(2):
         term_local(a).wait()
         for d in range(1, n_rep):
-            term_copy(a, d).wait_recv()
-            term_copy(a, d).wait_send()
+            if not pair:
+                term_copy(a, d).wait_recv()
+                term_copy(a, d).wait_send()
             weight_copy(a, d).wait_send()
         for j in range(1, SLICES):
-            raw_copy(a, j).wait_send()
+            for p in range(len(parts)):
+                raw_copy(a, j, p).wait_send()
 
         @pl.loop(1, planes)
         def _(k):
-            plane_copy(a, k).wait_send()
+            for p in range(len(parts)):
+                plane_copy(a, k, p).wait_send()
 
     for j in range(1, SLICES):
         place_copy(j).wait_send()
-        back_copy(j).wait_send()
         mate_copy(j).wait_send()
 
     @pl.loop(1, planes)
     def _(k):
-        dx_copy(k).wait_send()
+        for p in range(len(parts)):
+            dx_copy(k, p).wait_send()
         gate_copy(k).wait_send()
 
     @pl.loop(0, items)
@@ -418,6 +539,11 @@
         b_copy(s).wait_send()
         c_copy(s).wait_send()
         d_copy(s).wait_send()
+        if pair:
+            h_copy(s).wait_send()
+            f_copy(s).wait_send()
+            g_copy(s).wait_send()
+            y_copy(s // planes, s % planes).wait_send()
 
 
 def shards(tokens, cotangent, gates, routes, w_up, w_down_t):
@@ -431,22 +557,30 @@
     lanes = -(-slots // 128) * 128
     own_rows, hid = w_up.shape
     items = 2 * planes
+    pair = n_rep == 2
+    cover = max(
+        -(-(r + 1) * own_rows // 128) * 128 - r * own_rows // 128 * 128 for r in range(n_rep)
+    )
+    sums = 1 if pair else n_rep
+    peer = planes if pair else 1
+    n_parts = len(tiles(width, 512))
     dma = pltpu.SemaphoreType.DMA
     vmem = pl.BlockSpec(memory_space=pltpu.VMEM)
     hbm = pl.BlockSpec(memory_space=pl.ANY)
     pairs = []
     for shape in (
-        (2, SLICES), (SLICES,), (2, n_rep), (2, planes), (items,), (items,), (items,), (items,),
-        (planes,), (planes,), (2, n_rep), (SLICES,), (SLICES,),
+        (2, n_parts, SLICES), (SLICES,), (2, n_rep), (2, n_parts, planes), (items,), (items,), (items,), (items,),
+        (n_parts, planes), (planes,), (2, n_rep), (n_parts, SLICES), (SLICES,),
+        (2, planes), (items,), (items,), (items,),
     ):
         pairs += [dma(shape), dma(shape)]
     grad_tokens, gate_sums, up_sums, down_sums = pl.pallas_call(
-        functools.partial(kernel, n_rep, planes, capacity, slots),
+        functools.partial(kernel, n_rep, planes, capacity, slots, pair, cover),
         out_shape=(
             jax.ShapeDtypeStruct((tok_dev, model_width), BF16),
             jax.ShapeDtypeStruct((1, tok_dev), F32),
-            jax.ShapeDtypeStruct((n_rep, own_rows, hid), BF16),
-            jax.ShapeDtypeStruct((n_rep, own_rows, hid), BF16),
+            jax.ShapeDtypeStruct((sums, own_rows, hid), BF16),
+            jax.ShapeDtypeStruct((sums, own_rows, hid), BF16),
         ),
         in_specs=[hbm, hbm, vmem, vmem, hbm, hbm],
         out_specs=(hbm, vmem, hbm, hbm),
@@ -464,7 +598,7 @@
             pltpu.VMEM((items, slots, hid // 4), BF16),
             pltpu.VMEM((planes, slots, hid // 4), F32),
             pltpu.VMEM((items, slots, hid), BF16),
-            pltpu.VMEM((2, width, hid), BF16),
+            pltpu.VMEM((2, cover if pair else width, hid), BF16),
             pltpu.VMEM((planes, slots, width), BF16),
             pltpu.VMEM((planes, slots, width), BF16),
             pltpu.VMEM((planes, 8, lanes), F32),
@@ -472,6 +606,8 @@
             pltpu.VMEM((SLICES, tok_dev, width), BF16),
             pltpu.VMEM((SLICES, 8, tok_dev), F32),
             pltpu.VMEM((SLICES, 8, tok_dev), F32),
+            pltpu.VMEM((2, peer, slots, cover), BF16),
+            pltpu.VMEM((2 * peer, slots, hid), BF16),
             dma((5,)),
             *pairs,
         ],
@@ -482,8 +618,8 @@
             flops=12 * planes * slots * width * hid, bytes_accessed=8 * 1024 * 1024, transcendentals=0
         ),
     )(tokens, cotangent, gates.reshape(1, tok_dev), routes.reshape(1, tok_dev), w_up, w_down_t)
-    grad_up = sum(up_sums[d].astype(F32) for d in range(n_rep))
-    grad_down_t = sum(down_sums[d].astype(F32) for d in range(n_rep))
+    grad_up = sum(up_sums[d].astype(F32) for d in range(sums))
+    grad_down_t = sum(down_sums[d].astype(F32) for d in range(sums))
     return grad_tokens, gate_sums.reshape(tok_dev, top_count), grad_up, grad_down_t
 
 

time: 130 us -> 117 us (0.900)
  the two profiles are of different devices: /device:TPU:8 before, /device:TPU:0 now
where the time goes in v5:
time: 117 us
  Pallas kernels  111 us (95%)
  other arithmetic  3.78 us (3%)
  local copies, waits for them, and re-layouts  1.44 us (1%)
    pallas_call x1, Pallas kernels, shards(): pl.pallas_call(functools.partial(kernel, n_rep, planes, capacity, slots,...  111 us
    convert_element_type x1, other arithmetic, shards(): grad_down_t = sum((down_sums[d].astype(F32) for d in range(sums)))  3.78 us

profile of v5, /device:TPU:0, one launch (start us, length us, event | category | flops | bytes accessed | tf_op | source)
XLA Modules:
  0.0 116.7 jit_solution(3771542386161003004)
XLA Ops:
  0.6 110.9 %shard_map.93 = (bf16[128,3584]{1,0:T(8,128)(2,1)}, f32[1,128]{1,0:T(1,128)}, bf16[1,448,1024]{2,1,0:T(8,128)(2,1)}, bf16[1,448,1024]{2,1,0:T(8,128)(2,1)}) custom-call(bf16[128,3584]{1,0:T(8,128)(2,1)} %tokens.1, bf16[128,3584]{1,0:T(8,128)(2,1)} %cot.1, f32[1,128]{1,0:T(1,128)} %bitcast.9, s32[1,128]{1,0:T(1,128)} %bitcast.10, bf16[448,1024]{1,0:T(8,128)(2,1)} %w_up.1, ...), custom_call_target="tpu_custom_call" | custom-call | flops 6341787648 | bytes 8388608 | tf_op jit(solution)/shard_map/pallas_call | solution.py:577
  111.5 0.0 copy-start
  111.5 3.8 %bitcast_convert_fusion = (f32[448,1024]{1,0:T(8,128)}, f32[448,1024]{1,0:T(8,128)}) fusion(bf16[1,448,1024]{2,1,0:T(8,128)(2,1)} %get-tuple-element.11, bf16[1,448,1024]{2,1,0:T(8,128)(2,1)} %get-tuple-element.10), kind=kLoop, calls=%fused_computation | loop fusion | flops 917504 | bytes 5505024 | tf_op jit(solution)/shard_map/convert_element_type | solution.py:622
  115.3 0.0 copy-start.1
  115.3 0.0 copy-done
  115.3 0.9 copy.12
  116.2 0.0 copy-done.1
  116.2 0.5 copy.13
Async XLA Ops:
  111.5 3.8 %copy-start = (bf16[128,3584]{1,0:T(8,128)(2,1)S(1)}, bf16[128,3584]{1,0:T(8,128)(2,1)}, u32[]{:S(2)}) copy-start(bf16[128,3584]{1,0:T(8,128)(2,1)} %get-tuple-element.18) | copy-start | bytes 2752516
  115.3 0.9 copy-start.1

commit v6 on v5

--- a/solution.py
+++ b/solution.py
@@ -28,7 +28,7 @@
     grad_tokens, gate_sums, up_sums, down_sums,
     cot_block, out_grad, raw, place, weights, packed, rows, part, first, first_in, second_in,
     act, hidden, terms, dx, dx_in, gate_row, gate_in, back, gate_back, gate_mates,
-    rows_peer, hidden_peer,
+    rows_peer, hidden_peer, matrix,
     local_sem, raw_send, raw_recv, place_send, place_recv, weight_send, weight_recv,
     plane_send, plane_recv, a_send, a_recv, b_send, b_recv, c_send, c_recv, d_send, d_recv,
     dx_send, dx_recv, gate_send, gate_recv, term_send, term_recv, back_send, back_recv,
@@ -43,7 +43,8 @@
     items = 2 * planes
     hops = planes - 1
     parts = tiles(width, 512)
-    last_slot = planes + 2 * hops
+    early = 2 * hops
+    last_slot = early + 5
 
     def mate(distance):
         return (rep, plane * SLICES + (q + distance) % SLICES)
@@ -162,12 +163,12 @@
 
     def back_copy(j, p):
         return copy(
-            back.at[j, :, inner(p)], grad_tokens.at[:, feature_part(q, p)],
+            back.at[(q + j) % SLICES, :, inner(p)], grad_tokens.at[:, feature_part(q, p)],
             back_send.at[p, j], back_recv.at[p, j], mate(j),
         )
 
     def mate_copy(j):
-        return copy(gate_back.at[j], gate_mates.at[j], mate_send.at[j], mate_recv.at[j], mate(j))
+        return copy(gate_back.at[(q + j) % SLICES], gate_mates.at[j], mate_send.at[j], mate_recv.at[j], mate(j))
 
     def term_local(a):
         kept = weight_rows(rep)
@@ -236,17 +237,18 @@
         place_copy(j).wait_recv()
     places = jnp.concatenate([place[m, 0:1, :] for m in range(SLICES)], axis=1)
 
-    def chosen(expert, positions, kind):
-        number = lax.broadcasted_iota(jnp.int32, (slots, positions.shape[1]), 0) + expert * slots
-        return jnp.where(number.astype(F32) == positions, 1.0, 0.0).astype(kind)
+    @pl.loop(0, planes)
+    def _(k):
+        number = lax.broadcasted_iota(jnp.int32, (slots, SLICES * tok_dev), 0)
+        number = (number + (plane + k) % planes * slots).astype(F32)
+        matrix[k] = jnp.where(number == places, 1.0, 0.0).astype(BF16)
 
     def pack(a, k, p, target):
-        matrix = chosen((plane + k) % planes, places, BF16)
         begin, length = parts[p]
         for start, size in tiles(length):
             block = slice(begin + start, begin + start + size)
             source = raw[a, :, :, block].reshape(SLICES * tok_dev, size)
-            target[a, k, :, block] = dot(matrix, source, (1, 0)).astype(BF16)
+            target[a, k, :, block] = dot(matrix[k], source, (1, 0)).astype(BF16)
 
     for a in range(2):
         (local[0], local_grad)[a].wait()
@@ -263,7 +265,10 @@
             @pl.loop(1, planes)
             def _(k):
                 pack(a, k, p, packed)
-                plane_copy(a, k, p).start()
+
+                @pl.when(k < hops)
+                def _():
+                    plane_copy(a, k, p).start()
 
             pack(a, 0, p, rows)
         if pair:
@@ -271,12 +276,12 @@
     local[1].wait()
     local[2].wait()
 
-    def dx_product(k, p):
+    def dx_product(k, p, target):
         left = hidden[planes + k]
         begin, length = parts[p]
         for start, size in tiles(length):
             block = slice(begin + start, begin + start + size)
-            dx[k, :, block] = dot(left, weights[0, block, :], (1, 1)).astype(BF16)
+            target[k, :, block] = dot(left, weights[0, block, :], (1, 1)).astype(BF16)
 
     def split(value):
         upper = value.astype(BF16)
@@ -291,13 +296,37 @@
             term_copy(a, d).start()
         term_local(a).start()
 
-    @pl.loop(0, last_slot + (9 if pair else 6))
+    def pair_term(a):
+        @pl.loop((1 - a) * planes, (2 - a) * planes)
+        def _(t):
+            landed = hidden_peer.at[t, :, pl.ds(pl.multiple_of((1 - low) * half, 128), half)]
+            copy(landed, landed, g_send.at[t], g_recv.at[t], near).wait_recv()
+
+        @pl.loop(0, planes)
+        def _(k):
+            landed = rows_peer.at[a, k]
+            copy(landed, landed, y_send.at[a, k], y_recv.at[a, k], replica(1)).wait_recv()
+
+        count = planes * slots
+        mine = pl.ds(pl.multiple_of(cover_start(rep), 128), cover)
+        some = slice((1 - a) * planes, (2 - a) * planes)
+        total = dot(
+            rows[a, :, :, mine].reshape(count, cover), hidden[some].reshape(count, hid), (0, 0)
+        )
+        total += dot(
+            rows_peer[a].reshape(count, cover), hidden_peer[some].reshape(count, hid), (0, 0)
+        )
+        terms[a] = total.astype(BF16)
+        term_local(a).start()
+
+    @pl.loop(0, last_slot + (7 if pair else 5))
     def _(s):
         def stage(lag):
             slot = s - lag
-            extra = slot - planes
-            item = jnp.where(extra > 0, planes + extra // 2, slot)
-            return item, (slot >= 0) & (slot <= last_slot) & ((extra <= 0) | (extra % 2 == 0))
+            item = jnp.where(slot < hops, slot, slot + 1)
+            item = jnp.where(slot < early, item, (slot - early - 3) * planes - 1)
+            here = (slot >= 0) & (slot <= last_slot)
+            return item, here & ((slot < early) | (slot >= early + 4))
 
         e_item, e_here = stage(4)
 
@@ -310,12 +339,17 @@
             @pl.when(t >= planes)
             def _():
                 k = t - planes
-                dx_product(k, 0)
+                @pl.when(k == 0)
+                def _():
+                    for p in range(len(parts)):
+                        dx_product(0, p, dx_in)
 
                 @pl.when(k > 0)
                 def _():
                     gate_copy(k).start()
-                    dx_copy(k, 0).start()
+                    for p in range(len(parts)):
+                        dx_product(k, p, dx)
+                        dx_copy(k, p).start()
 
         d_item, d_here = stage(3)
 
@@ -394,6 +428,12 @@
                 if pair:
                     y_copy(a, k).start()
 
+            @pl.when(i == items - 3)
+            def _():
+                for b in range(2):
+                    for p in range(len(parts)):
+                        plane_copy(b, hops, p).start()
+
             left = rows[a, k]
             for start, size in tiles(hid):
                 part[i, :, start : start + size] = dot(
@@ -401,25 +441,15 @@
                 ).astype(BF16)
             a_copy(i).start()
 
-        @pl.when(s == last_slot + 5)
-        def _():
-            for p in range(1, len(parts)):
-                dx_product(0, p)
-
-                @pl.loop(1, planes)
-                def _(k):
-                    dx_product(k, p)
-                    dx_copy(k, p).start()
-
         if pair:
-            f_item, f_here = stage(6)
+            f_item, f_here = stage(5)
 
             @pl.when(f_here)
             def _():
                 h_copy(f_item).wait_recv()
                 f_copy(f_item).start()
 
-            g_item, g_here = stage(8)
+            g_item, g_here = stage(6)
 
             @pl.when(g_here)
             def _():
@@ -429,39 +459,16 @@
                 ]
                 copy(landed, landed, f_send.at[t], f_recv.at[t], far).wait_recv()
                 g_copy(t).start()
+
+            @pl.when(s == last_slot + 5)
+            def _():
+                pair_term(1)
         else:
-            @pl.when(s == last_slot + 1)
+            @pl.when(s == last_slot + 3)
             def _():
                 weight_term(1)
 
-    def pair_term(a):
-        @pl.loop((1 - a) * planes, (2 - a) * planes)
-        def _(t):
-            landed = hidden_peer.at[t, :, pl.ds(pl.multiple_of((1 - low) * half, 128), half)]
-            copy(landed, landed, g_send.at[t], g_recv.at[t], near).wait_recv()
-
-        @pl.loop(0, planes)
-        def _(k):
-            landed = rows_peer.at[a, k]
-            copy(landed, landed, y_send.at[a, k], y_recv.at[a, k], replica(1)).wait_recv()
-
-        count = planes * slots
-        mine = pl.ds(pl.multiple_of(cover_start(rep), 128), cover)
-        some = slice((1 - a) * planes, (2 - a) * planes)
-        total = dot(
-            rows[a, :, :, mine].reshape(count, cover), hidden[some].reshape(count, hid), (0, 0)
-        )
-        total += dot(
-            rows_peer[a].reshape(count, cover), hidden_peer[some].reshape(count, hid), (0, 0)
-        )
-        terms[a] = total.astype(BF16)
-        term_local(a).start()
-
-    if pair:
-        pair_term(1)
-        pair_term(0)
-    else:
-        weight_term(0)
+    (pair_term if pair else weight_term)(0)
 
     @pl.loop(1, planes)
     def _(k):
@@ -472,31 +479,27 @@
         def _(k):
             dx_copy(k, p).wait_recv()
 
-        for j in (2, 1, 3, 0):
-            positions = place[(q + j) % SLICES][0:1, :]
-            blocks = [chosen((plane + k) % planes, positions, BF16) for k in range(planes)]
-            matrix = jnp.concatenate(blocks, axis=0)
-            landed = jnp.concatenate(
-                [dx[0, :, inner(p)]] + [dx_in[k, :, inner(p)] for k in range(1, planes)], axis=0
-            )
-            back[j, :, inner(p)] = dot(matrix, landed, (0, 0)).astype(BF16)
-            if j > 0:
-                back_copy(j, p).start()
-            if p > 0:
-                continue
-            sums = jnp.zeros((8, tok_dev), F32)
+        every = matrix[...].reshape(planes * slots, SLICES * tok_dev)
+        landed = dx_in[:, :, inner(p)].reshape(planes * slots, parts[p][1])
+        token_rows = dot(every, landed, (0, 0)).astype(BF16)
+        back[:, :, inner(p)] = token_rows.reshape(SLICES, tok_dev, parts[p][1])
+        for j in (2, 1, 3):
+            back_copy(j, p).start()
+        if p == 0:
+            sums = jnp.zeros((8, SLICES * tok_dev), F32)
             for k in range(planes):
                 upper, lower = split((gate_row if k == 0 else gate_in)[k, :, 0:slots])
-                both = dot(jnp.concatenate([upper, lower], axis=0), blocks[k], (1, 0))
+                both = dot(jnp.concatenate([upper, lower], axis=0), matrix[k], (1, 0))
                 sums += both[0:8] + both[8:16]
-            gate_back[j] = sums
-            if j > 0:
+            for m in range(SLICES):
+                gate_back[m] = sums[:, m * tok_dev : (m + 1) * tok_dev]
+            for j in range(1, SLICES):
                 mate_copy(j).start()
     last = pltpu.make_async_copy(
-        back.at[0], grad_tokens.at[:, feature_block(q)], local_sem.at[2]
+        back.at[q], grad_tokens.at[:, feature_block(q)], local_sem.at[2]
     )
     last.start()
-    total = gate_back[0]
+    total = gate_back[q]
     for j in range(1, SLICES):
         mate_copy(j).wait_recv()
         total += gate_mates[j]
@@ -608,6 +611,7 @@
             pltpu.VMEM((SLICES, 8, tok_dev), F32),
             pltpu.VMEM((2, peer, slots, cover), BF16),
             pltpu.VMEM((2 * peer, slots, hid), BF16),
+            pltpu.VMEM((planes, slots, SLICES * tok_dev), BF16),
             dma((5,)),
             *pairs,
         ],

time: 117 us -> 126 us (1.077)
  Pallas kernels: 111 us -> 120 us
    pallas_call x1, Pallas kernels: 111 us -> 120 us  [shards(): pl.pallas_call(functools.partial(kernel, n_rep, planes, capacity, slots,...]
where the time goes in v6:
time: 126 us; the launch traced here: 125 us
  Pallas kernels  120 us (95%)
  other arithmetic  3.78 us (3%)
  local copies, waits for them, and re-layouts  1.44 us (1%)
    pallas_call x1, Pallas kernels, shards(): pl.pallas_call(functools.partial(kernel, n_rep, planes, capacity, slots,...  120 us
    convert_element_type x1, other arithmetic, shards(): grad_down_t = sum((down_sums[d].astype(F32) for d in range(sums)))  3.78 us

profile of v6, /device:TPU:0, one launch (start us, length us, event | category | flops | bytes accessed | tf_op | source)
XLA Modules:
  0.0 125.4 jit_solution(7009612195381699882)
XLA Ops:
  0.6 119.5 %shard_map.93 = (bf16[128,3584]{1,0:T(8,128)(2,1)}, f32[1,128]{1,0:T(1,128)}, bf16[1,448,1024]{2,1,0:T(8,128)(2,1)}, bf16[1,448,1024]{2,1,0:T(8,128)(2,1)}) custom-call(bf16[128,3584]{1,0:T(8,128)(2,1)} %tokens.1, bf16[128,3584]{1,0:T(8,128)(2,1)} %cot.1, f32[1,128]{1,0:T(1,128)} %bitcast.9, s32[1,128]{1,0:T(1,128)} %bitcast.10, bf16[448,1024]{1,0:T(8,128)(2,1)} %w_up.1, ...), custom_call_target="tpu_custom_call" | custom-call | flops 6341787648 | bytes 8388608 | tf_op jit(solution)/shard_map/pallas_call | solution.py:580
  120.1 0.0 copy-start
  120.2 3.8 %bitcast_convert_fusion = (f32[448,1024]{1,0:T(8,128)}, f32[448,1024]{1,0:T(8,128)}) fusion(bf16[1,448,1024]{2,1,0:T(8,128)(2,1)} %get-tuple-element.11, bf16[1,448,1024]{2,1,0:T(8,128)(2,1)} %get-tuple-element.10), kind=kLoop, calls=%fused_computation | loop fusion | flops 917504 | bytes 5505024 | tf_op jit(solution)/shard_map/convert_element_type | solution.py:626
  123.9 0.0 copy-start.1
  123.9 0.0 copy-done
  123.9 0.9 copy.12
  124.9 0.0 copy-done.1
  124.9 0.5 copy.13
Async XLA Ops:
  120.1 3.8 %copy-start = (bf16[128,3584]{1,0:T(8,128)(2,1)S(1)}, bf16[128,3584]{1,0:T(8,128)(2,1)}, u32[]{:S(2)}) copy-start(bf16[128,3584]{1,0:T(8,128)(2,1)} %get-tuple-element.18) | copy-start | bytes 2752516
  123.9 0.9 copy-start.1

commit v7 on v6

--- a/solution.py
+++ b/solution.py
@@ -41,10 +41,8 @@
     own_rows, hid = w_up.shape
     half, quarter = hid // 2, hid // 4
     items = 2 * planes
-    hops = planes - 1
     parts = tiles(width, 512)
-    early = 2 * hops
-    last_slot = early + 5
+    last_slot = items - 1
 
     def mate(distance):
         return (rep, plane * SLICES + (q + distance) % SLICES)
@@ -265,10 +263,7 @@
             @pl.loop(1, planes)
             def _(k):
                 pack(a, k, p, packed)
-
-                @pl.when(k < hops)
-                def _():
-                    plane_copy(a, k, p).start()
+                plane_copy(a, k, p).start()
 
             pack(a, 0, p, rows)
         if pair:
@@ -319,14 +314,10 @@
         terms[a] = total.astype(BF16)
         term_local(a).start()
 
-    @pl.loop(0, last_slot + (7 if pair else 5))
+    @pl.loop(0, last_slot + (7 if pair else 6))
     def _(s):
         def stage(lag):
-            slot = s - lag
-            item = jnp.where(slot < hops, slot, slot + 1)
-            item = jnp.where(slot < early, item, (slot - early - 3) * planes - 1)
-            here = (slot >= 0) & (slot <= last_slot)
-            return item, here & ((slot < early) | (slot >= early + 4))
+            return s - lag, (s >= lag) & (s <= last_slot + lag)
 
         e_item, e_here = stage(4)
 
@@ -346,10 +337,9 @@
 
                 @pl.when(k > 0)
                 def _():
+                    dx_product(k, 0, dx)
+                    dx_copy(k, 0).start()
                     gate_copy(k).start()
-                    for p in range(len(parts)):
-                        dx_product(k, p, dx)
-                        dx_copy(k, p).start()
 
         d_item, d_here = stage(3)
 
@@ -428,12 +418,6 @@
                 if pair:
                     y_copy(a, k).start()
 
-            @pl.when(i == items - 3)
-            def _():
-                for b in range(2):
-                    for p in range(len(parts)):
-                        plane_copy(b, hops, p).start()
-
             left = rows[a, k]
             for start, size in tiles(hid):
                 part[i, :, start : start + size] = dot(
@@ -441,6 +425,14 @@
                 ).astype(BF16)
             a_copy(i).start()
 
+        @pl.when(s == last_slot + 5)
+        def _():
+            for p in range(1, len(parts)):
+                @pl.loop(1, planes)
+                def _(k):
+                    dx_product(k, p, dx)
+                    dx_copy(k, p).start()
+
         if pair:
             f_item, f_here = stage(5)
 
@@ -460,7 +452,7 @@
                 copy(landed, landed, f_send.at[t], f_recv.at[t], far).wait_recv()
                 g_copy(t).start()
 
-            @pl.when(s == last_slot + 5)
+            @pl.when(s == last_slot + 6)
             def _():
                 pair_term(1)
         else:

time: 126 us -> 114 us (0.905)
  Pallas kernels: 120 us -> 107 us
    pallas_call x1, Pallas kernels: 120 us -> 107 us  [shards(): pl.pallas_call(functools.partial(kernel, n_rep, planes, capacity, slots,...]
where the time goes in v7:
time: 114 us; the launch traced here: 113 us
  Pallas kernels  107 us (94%)
  other arithmetic  3.78 us (3%)
  local copies, waits for them, and re-layouts  1.44 us (1%)
    pallas_call x1, Pallas kernels, shards(): pl.pallas_call(functools.partial(kernel, n_rep, planes, capacity, slots,...  107 us
    convert_element_type x1, other arithmetic, shards(): grad_down_t = sum((down_sums[d].astype(F32) for d in range(sums)))  3.78 us

profile of v7, /device:TPU:0, one launch (start us, length us, event | category | flops | bytes accessed | tf_op | source)
XLA Modules:
  0.0 113.3 jit_solution(4746388505609556934)
XLA Ops:
  0.6 107.4 %shard_map.93 = (bf16[128,3584]{1,0:T(8,128)(2,1)}, f32[1,128]{1,0:T(1,128)}, bf16[1,448,1024]{2,1,0:T(8,128)(2,1)}, bf16[1,448,1024]{2,1,0:T(8,128)(2,1)}) custom-call(bf16[128,3584]{1,0:T(8,128)(2,1)} %tokens.1, bf16[128,3584]{1,0:T(8,128)(2,1)} %cot.1, f32[1,128]{1,0:T(1,128)} %bitcast.9, s32[1,128]{1,0:T(1,128)} %bitcast.10, bf16[448,1024]{1,0:T(8,128)(2,1)} %w_up.1, ...), custom_call_target="tpu_custom_call" | custom-call | flops 6341787648 | bytes 8388608 | tf_op jit(solution)/shard_map/pallas_call | solution.py:572
  108.0 0.0 copy-start
  108.0 3.8 %bitcast_convert_fusion = (f32[448,1024]{1,0:T(8,128)}, f32[448,1024]{1,0:T(8,128)}) fusion(bf16[1,448,1024]{2,1,0:T(8,128)(2,1)} %get-tuple-element.11, bf16[1,448,1024]{2,1,0:T(8,128)(2,1)} %get-tuple-element.10), kind=kLoop, calls=%fused_computation | loop fusion | flops 917504 | bytes 5505024 | tf_op jit(solution)/shard_map/convert_element_type | solution.py:618
  111.8 0.0 copy-start.1
  111.8 0.0 copy-done
  111.8 0.9 copy.12
  112.8 0.0 copy-done.1
  112.8 0.5 copy.13
Async XLA Ops:
  108.0 3.8 %copy-start = (bf16[128,3584]{1,0:T(8,128)(2,1)S(1)}, bf16[128,3584]{1,0:T(8,128)(2,1)}, u32[]{:S(2)}) copy-start(bf16[128,3584]{1,0:T(8,128)(2,1)} %get-tuple-element.18) | copy-start | bytes 2752516
  111.8 0.9 copy-start.1

commit v8 on v7

--- a/solution.py
+++ b/solution.py
@@ -460,7 +460,8 @@
             def _():
                 weight_term(1)
 
-    (pair_term if pair else weight_term)(0)
+    if not pair:
+        weight_term(0)
 
     @pl.loop(1, planes)
     def _(k):
@@ -487,6 +488,8 @@
                 gate_back[m] = sums[:, m * tok_dev : (m + 1) * tok_dev]
             for j in range(1, SLICES):
                 mate_copy(j).start()
+            if pair:
+                pair_term(0)
     last = pltpu.make_async_copy(
         back.at[q], grad_tokens.at[:, feature_block(q)], local_sem.at[2]
     )

time: 114 us -> 114 us (level)
  no operation moved by 1% of the time
where the time goes in v8:
time: 114 us; the launch traced here: 113 us
  Pallas kernels  107 us (94%)
  other arithmetic  3.78 us (3%)
  local copies, waits for them, and re-layouts  1.44 us (1%)
    pallas_call x1, Pallas kernels, shards(): pl.pallas_call(functools.partial(kernel, n_rep, planes, capacity, slots,...  107 us
    convert_element_type x1, other arithmetic, shards(): grad_down_t = sum((down_sums[d].astype(F32) for d in range(sums)))  3.78 us

profile of v8, /device:TPU:0, one launch (start us, length us, event | category | flops | bytes accessed | tf_op | source)
XLA Modules:
  0.0 113.0 jit_solution(6518701056026663642)
XLA Ops:
  0.6 107.2 %shard_map.93 = (bf16[128,3584]{1,0:T(8,128)(2,1)}, f32[1,128]{1,0:T(1,128)}, bf16[1,448,1024]{2,1,0:T(8,128)(2,1)}, bf16[1,448,1024]{2,1,0:T(8,128)(2,1)}) custom-call(bf16[128,3584]{1,0:T(8,128)(2,1)} %tokens.1, bf16[128,3584]{1,0:T(8,128)(2,1)} %cot.1, f32[1,128]{1,0:T(1,128)} %bitcast.9, s32[1,128]{1,0:T(1,128)} %bitcast.10, bf16[448,1024]{1,0:T(8,128)(2,1)} %w_up.1, ...), custom_call_target="tpu_custom_call" | custom-call | flops 6341787648 | bytes 8388608 | tf_op jit(solution)/shard_map/pallas_call | solution.py:575
  107.8 0.0 copy-start
  107.8 3.8 %bitcast_convert_fusion = (f32[448,1024]{1,0:T(8,128)}, f32[448,1024]{1,0:T(8,128)}) fusion(bf16[1,448,1024]{2,1,0:T(8,128)(2,1)} %get-tuple-element.11, bf16[1,448,1024]{2,1,0:T(8,128)(2,1)} %get-tuple-element.10), kind=kLoop, calls=%fused_computation | loop fusion | flops 917504 | bytes 5505024 | tf_op jit(solution)/shard_map/convert_element_type | solution.py:621
  111.6 0.0 copy-start.1
  111.6 0.0 copy-done
  111.6 0.9 copy.12
  112.5 0.0 copy-done.1
  112.5 0.5 copy.13
Async XLA Ops:
  107.8 3.8 %copy-start = (bf16[128,3584]{1,0:T(8,128)(2,1)S(1)}, bf16[128,3584]{1,0:T(8,128)(2,1)}, u32[]{:S(2)}) copy-start(bf16[128,3584]{1,0:T(8,128)(2,1)} %get-tuple-element.18) | copy-start | bytes 2752516
  111.6 0.9 copy-start.1
